TPU v7x, 128 devices: a whole 4x4x4 slice. The times are simulated.
128 devices in a mesh: dp: 8 (over x, core), ctx: 16 (over y, z).
Axes of the slice: x: 4, y: 4, z: 4, core: 2. Of those that a mesh axis runs over, the one named last changes fastest.
Arguments:
- layer_input: bfloat16 [16384, 6144], P(('dp', 'ctx')), may hold values from -24 to 24
- query_rows: bfloat16 [16384, 4096], P(('dp', 'ctx')), may hold values from -5 to 5
- key_rows: bfloat16 [16384, 4096], P(('dp', 'ctx')), may hold values from -5 to 5
- value_rows: bfloat16 [16384, 4096], P(('dp', 'ctx')), may hold values from -6 to 6
- out_grad: bfloat16 [16384, 4096], P(('dp', 'ctx')), may hold values from -6 to 6
- doc_lengths: int32 [8, 16], P('dp'), may hold values from 1 to 1024, 2048 in all within a row
- dilations: int32 [16], replicated, may hold values from 2 to 8, as said below
- seg_lengths: int32 [16], replicated, may hold values from 256 to 2048, as said below
Outputs:
- attention_out: bfloat16 [16384, 4096], P(('dp', 'ctx'))
- grad_query: bfloat16 [16384, 4096], P(('dp', 'ctx'))
- grad_key: bfloat16 [16384, 4096], P(('dp', 'ctx'))
- grad_value: bfloat16 [16384, 4096], P(('dp', 'ctx'))
- weight_grad: float32 [6144, 3, 4096], P('dp', None, 'ctx')
Inputs may be any that keep to these rules, and one draw needn't show every extreme that they name: `dilations`: each rate is 2, 4 or 8; in every draw some head group has rate 2. `seg_lengths`: each segment length is 2048 divided by 1, 2, 4 or 8.
All inputs are finite; a program needn't handle non-finite values.
Results may differ from a plain program's by a relative error of at most 0.015.
Values may be sent and summed in bfloat16 or wider, within the bound.
A program may use at most 128 MiB of HBM per device.

v0:
```python
import math

import jax
import jax.numpy as jnp
from jax import lax
from jax.sharding import PartitionSpec as P

HS = 128


def attend(queries, keys, values, cotangent, position, usable, doc_id, segment):
    count = queries.shape[0]
    query_heads = queries.reshape(count, -1, HS)
    key_heads = keys.reshape(count, -1, HS)
    value_heads = values.reshape(count, -1, HS)
    grad_heads = cotangent.reshape(count, -1, HS)
    slot_ids = jnp.arange(count, dtype=jnp.int32)
    allowed = (
        usable[:, None]
        & usable[None, :]
        & (doc_id[:, None] == doc_id[None, :])
        & (segment[:, None] == segment[None, :])
        & (position[None, :] <= position[:, None])
    )
    allowed = allowed | (slot_ids[:, None] == slot_ids[None, :])
    score_scale = 1.0 / math.sqrt(HS)
    scores = (
        jnp.einsum("qhd,khd->hqk", query_heads, key_heads, preferred_element_type=jnp.float32)
        * score_scale
    )
    scores = jnp.where(allowed[None], scores, -1e30)
    row_max = jnp.max(scores, axis=2, keepdims=True)
    expos = jnp.exp(scores - row_max)
    probs = expos / jnp.sum(expos, axis=2, keepdims=True)
    weights = probs.astype(jnp.bfloat16)
    result = jnp.einsum(
        "hqk,khd->qhd", weights, value_heads, preferred_element_type=jnp.float32
    ).astype(jnp.bfloat16)
    dprob = jnp.einsum("qhd,khd->hqk", grad_heads, value_heads, preferred_element_type=jnp.float32)
    delta = jnp.sum(probs * dprob, axis=2, keepdims=True)
    dscore = (probs * (dprob - delta) * score_scale).astype(jnp.bfloat16)
    grad_q = jnp.einsum(
        "hqk,khd->qhd", dscore, key_heads, preferred_element_type=jnp.float32
    ).astype(jnp.bfloat16)
    grad_k = jnp.einsum(
        "hqk,qhd->khd", dscore, query_heads, preferred_element_type=jnp.float32
    ).astype(jnp.bfloat16)
    grad_v = jnp.einsum(
        "hqk,qhd->khd", weights, grad_heads, preferred_element_type=jnp.float32
    ).astype(jnp.bfloat16)
    return (
        result.reshape(count, -1),
        grad_q.reshape(count, -1),
        grad_k.reshape(count, -1),
        grad_v.reshape(count, -1),
    )


def on_device(
    layer_input, query_rows, key_rows, value_rows, out_grad, doc_lengths, dilations, seg_lengths
):
    tokens_here = layer_input.shape[0]
    width = query_rows.shape[1]
    groups = dilations.shape[0]
    group_width = width // groups
    ctx_count = lax.axis_size("ctx")
    dp_count = lax.axis_size("dp")
    device = lax.axis_index("ctx")
    owned = groups // ctx_count
    capacity = tokens_here // 2
    pack_length = tokens_here * ctx_count
    slot_count = ctx_count * capacity
    group_ids = jnp.arange(groups, dtype=jnp.int32)
    offsets = group_ids % dilations
    slot = jnp.arange(capacity, dtype=jnp.int32)
    row_ids = jnp.arange(tokens_here, dtype=jnp.int32)
    taken = slot[None, :] < (tokens_here // dilations)[:, None]
    local_rows = offsets[:, None] + dilations[:, None] * slot[None, :]
    local_select = (taken[:, :, None] & (local_rows[:, :, None] == row_ids[None, None, :])).astype(
        jnp.bfloat16
    )
    input_taken = jnp.einsum(
        "gst,td->gsd", local_select, layer_input, preferred_element_type=jnp.float32
    ).astype(jnp.bfloat16)
    shaped = [
        tensor.reshape(tokens_here, groups, group_width)
        for tensor in (query_rows, key_rows, value_rows, out_grad)
    ]
    owned_ids = device * owned + jnp.arange(owned, dtype=jnp.int32)
    owned_rates = jnp.take(dilations, owned_ids)
    owned_offsets = owned_ids % owned_rates
    owned_segments = jnp.take(seg_lengths, owned_ids)
    every_slot = jnp.arange(slot_count, dtype=jnp.int32)
    source = every_slot // capacity
    within = every_slot % capacity
    position = (
        source[None, :] * tokens_here
        + owned_offsets[:, None]
        + owned_rates[:, None] * within[None, :]
    )
    usable = within[None, :] < (tokens_here // owned_rates)[:, None]
    doc_ends = jnp.cumsum(doc_lengths[0], dtype=jnp.int32)
    doc_id = jnp.sum((position[:, :, None] >= doc_ends[None, None, :]).astype(jnp.int32), axis=2)
    segment = position // owned_segments[:, None]
    q_dense, k_dense, v_dense, g_dense = (
        lax.all_to_all(shaped[0], "ctx", split_axis=1, concat_axis=0, tiled=True),
        lax.all_to_all(shaped[1], "ctx", split_axis=1, concat_axis=0, tiled=True),
        lax.all_to_all(shaped[2], "ctx", split_axis=1, concat_axis=0, tiled=True),
        lax.all_to_all(shaped[3], "ctx", split_axis=1, concat_axis=0, tiled=True),
    )
    input_slots = lax.all_to_all(input_taken, "ctx", split_axis=0, concat_axis=1, tiled=True)
    pack_ids = jnp.arange(pack_length, dtype=jnp.int32)
    owner_select = (usable[:, :, None] & (position[:, :, None] == pack_ids[None, None, :])).astype(
        jnp.bfloat16
    )
    selected = [
        jnp.einsum("gsp,pgc->gsc", owner_select, tensor, preferred_element_type=jnp.float32).astype(
            jnp.bfloat16
        )
        for tensor in (q_dense, k_dense, v_dense, g_dense)
    ]
    q_slots, k_slots, v_slots, g_slots = selected

    def per_group(item):
        return attend(item[0], item[1], item[2], item[3], item[4], item[5], item[6], item[7])

    results, grads_q, grads_k, grads_v = lax.map(
        per_group, (q_slots, k_slots, v_slots, g_slots, position, usable, doc_id, segment)
    )
    stacked = jnp.stack([grads_q, grads_k, grads_v], axis=2)
    grad_scale = 1.0 / math.sqrt(pack_length * dp_count)
    product = jnp.einsum("gsd,gstc->dtgc", input_slots, stacked, preferred_element_type=jnp.float32)
    weight_grad = lax.psum_scatter(
        (
            product.reshape(
                input_slots.shape[2] // dp_count * lax.axis_size("dp"), 3, owned * group_width
            )
            * grad_scale
        ).astype(jnp.bfloat16),
        "dp",
        scatter_dimension=0,
        tiled=True,
    ).astype(jnp.float32)
    spread = [
        jnp.einsum("gsp,gsc->pgc", owner_select, tensor, preferred_element_type=jnp.float32).astype(
            jnp.bfloat16
        )
        for tensor in (results, grads_q, grads_k, grads_v)
    ]
    returned = (
        lax.all_to_all(spread[0], "ctx", split_axis=0, concat_axis=1, tiled=True),
        lax.all_to_all(spread[1], "ctx", split_axis=0, concat_axis=1, tiled=True),
        lax.all_to_all(spread[2], "ctx", split_axis=0, concat_axis=1, tiled=True),
        lax.all_to_all(spread[3], "ctx", split_axis=0, concat_axis=1, tiled=True),
    )
    outputs = [tensor.reshape(tokens_here, width) for tensor in returned]
    return (outputs[0], outputs[1], outputs[2], outputs[3], weight_grad)


def solution(mesh):
    return jax.shard_map(
        on_device,
        mesh=mesh,
        in_specs=(
            P(("dp", "ctx"), None),
            P(("dp", "ctx"), None),
            P(("dp", "ctx"), None),
            P(("dp", "ctx"), None),
            P(("dp", "ctx"), None),
            P("dp", None),
            P(),
            P(),
        ),
        out_specs=(
            P(("dp", "ctx"), None),
            P(("dp", "ctx"), None),
            P(("dp", "ctx"), None),
            P(("dp", "ctx"), None),
            P("dp", None, "ctx"),
        ),
        check_vma=False,
    )
```

profile of v0, /device:TPU:8, one launch (start us, length us, event | category | flops | bytes accessed | tf_op | source)
XLA Modules:
  0.0 435.3 jit_solution(4684627243649713663)
XLA Ops:
  9.6 8.4 %all-to-all-start.1 = ((bf16[128,16,256]{0,2,1:T(8,128)(2,1)}), bf16[128,16,256]{0,2,1:T(8,128)(2,1)S(1)}, u32[]{:S(2)}, u32[]{:S(2)}) async-start(bf16[128,16,256]{0,2,1:T(8,128)(2,1)} %bitcast.158), calls=%async_computation.1 | async-start | bytes 2097152 | tf_op jit(solution)/shard_map/all_to_all | solution.py:106
  20.2 12.8 %all-to-all-done.1 = bf16[128,16,256]{0,2,1:T(8,128)(2,1)S(1)} async-done(((bf16[128,16,256]{0,2,1:T(8,128)(2,1)}), bf16[128,16,256]{0,2,1:T(8,128)(2,1)S(1)}, u32[]{:S(2)}, u32[]{:S(2)}) %all-to-all-start.1) | async-done | bytes 1048608 | tf_op jit(solution)/shard_map/all_to_all | solution.py:106
  33.0 6.8 %all-to-all-start.2 = ((bf16[128,16,256]{0,2,1:T(8,128)(2,1)}), bf16[128,16,256]{0,2,1:T(8,128)(2,1)}, u32[]{:S(2)}, u32[]{:S(2)}) async-start(bf16[128,16,256]{0,2,1:T(8,128)(2,1)} %bitcast.157), calls=%async_computation.2 | async-start | bytes 2097152 | tf_op jit(solution)/shard_map/all_to_all | solution.py:107
  42.1 10.7 %all-to-all-done.2 = bf16[128,16,256]{0,2,1:T(8,128)(2,1)} async-done(((bf16[128,16,256]{0,2,1:T(8,128)(2,1)}), bf16[128,16,256]{0,2,1:T(8,128)(2,1)}, u32[]{:S(2)}, u32[]{:S(2)}) %all-to-all-start.2) | async-done | bytes 1048608 | tf_op jit(solution)/shard_map/all_to_all | solution.py:107
  52.8 6.5 %all-to-all-start = ((bf16[128,16,256]{0,2,1:T(8,128)(2,1)}), bf16[128,16,256]{0,2,1:T(8,128)(2,1)}, u32[]{:S(2)}, u32[]{:S(2)}) async-start(bf16[128,16,256]{0,2,1:T(8,128)(2,1)} %bitcast.156), calls=%async_computation | async-start | bytes 2097152 | tf_op jit(solution)/shard_map/all_to_all | solution.py:108
  61.7 10.4 %all-to-all-done = bf16[128,16,256]{0,2,1:T(8,128)(2,1)} async-done(((bf16[128,16,256]{0,2,1:T(8,128)(2,1)}), bf16[128,16,256]{0,2,1:T(8,128)(2,1)}, u32[]{:S(2)}, u32[]{:S(2)}) %all-to-all-start) | async-done | bytes 1048608 | tf_op jit(solution)/shard_map/all_to_all | solution.py:108
  72.1 6.2 %all-to-all-start.4 = ((bf16[128,16,256]{0,2,1:T(8,128)(2,1)}), bf16[128,16,256]{0,2,1:T(8,128)(2,1)}, u32[]{:S(2)}, u32[]{:S(2)}) async-start(bf16[128,16,256]{0,2,1:T(8,128)(2,1)} %bitcast.155), calls=%async_computation.4 | async-start | bytes 2097152 | tf_op jit(solution)/shard_map/all_to_all | solution.py:109
  78.4 6.4 %convolution_convert_fusion = bf16[16,64,6144]{2,1,0:T(8,128)(2,1)} fusion(bf16[128,6144]{1,0:T(8,128)(2,1)S(1)} %copy-done, s32[16,64]{1,0:T(8,128)S(1)} %multiply_add_fusion, pred[16,64]{1,0:T(8,128)(4,1)S(1)} %iota_compare_fusion.3), kind=kOutput, calls=%fused_computation.3 | convolution fusion | flops 1617166336 | bytes 14160896 | tf_op jit(solution)/shard_map/gst,td->gsd/dot_general | solution.py:82
  84.8 6.3 %all-to-all-done.4 = bf16[128,16,256]{0,2,1:T(8,128)(2,1)} async-done(((bf16[128,16,256]{0,2,1:T(8,128)(2,1)}), bf16[128,16,256]{0,2,1:T(8,128)(2,1)}, u32[]{:S(2)}, u32[]{:S(2)}) %all-to-all-start.4) | async-done | bytes 1048608 | tf_op jit(solution)/shard_map/all_to_all | solution.py:109
  91.1 6.8 %all-to-all-start.8 = ((bf16[16,64,6144]{2,1,0:T(8,128)(2,1)}), bf16[16,64,6144]{2,1,0:T(8,128)(2,1)}, u32[]{:S(2)}, u32[]{:S(2)}) async-start(bf16[16,64,6144]{2,1,0:T(8,128)(2,1)} %convolution_convert_fusion), calls=%async_computation.8 | async-start | bytes 25165824 | tf_op jit(solution)/shard_map/all_to_all | solution.py:111
  124.9 4.5 %fusion.132 = f32[2,1024,1024]{1,2,0:T(8,128)} fusion(bf16[1024,2,128]{0,2,1:T(8,128)(2,1)S(1)} %bitcast.169, bf16[1024,2,128]{0,2,1:T(8,128)(2,1)S(1)} %bitcast.167), kind=kOutput, calls=%fused_computation.109 | convolution fusion | flops 536870912 | bytes 9437184 | tf_op jit(solution)/shard_map/while/body/eval_jaxpr/qhd,khd->hqk/dot_general | solution.py:39
  129.4 5.4 %fusion.131 = (f32[2,1024]{1,0:T(2,128)S(1)}, f32[2,1024,1024]{1,2,0:T(8,128)}) fusion(pred[1024,1024]{0,1:T(8,128)(4,1)S(1)} %fusion.43, bf16[1024,2,128]{0,2,1:T(8,128)(2,1)S(1)} %bitcast.178, bf16[1024,2,128]{0,2,1:T(8,128)(2,1)S(1)} %bitcast.180), kind=kOutput, calls=%fused_computation.108 | convolution fusion | flops 545260544 | bytes 10493952 | tf_op jit(solution)/shard_map/while/body/eval_jaxpr/sub | solution.py:33
  134.8 13.6 %fusion.102 = bf16[2,128,1024]{2,1,0:T(8,128)(2,1)S(1)} fusion(bf16[1024,2,128]{0,2,1:T(8,128)(2,1)S(1)} %bitcast.181, f32[2,1024,1024]{1,2,0:T(8,128)} %fusion.132, f32[2,1024,1024]{1,2,0:T(8,128)} %get-tuple-element.104, f32[2,1024]{1,0:T(2,128)S(1)} %get-tuple-element.103), kind=kOutput, calls=%fused_computation.70 | convolution fusion | flops 551816192 | bytes 17833984 | tf_op jit(solution)/shard_map/while/body/eval_jaxpr/hqk,khd->qhd/dot_general | solution.py:42
  148.4 12.4 %fusion.105 = bf16[2,128,1024]{2,1,0:T(8,128)(2,1)S(1)} fusion(bf16[1024,2,128]{0,2,1:T(8,128)(2,1)S(1)} %bitcast.179, f32[2,1024,1024]{1,2,0:T(8,128)} %fusion.132, f32[2,1024,1024]{1,2,0:T(8,128)} %get-tuple-element.104, f32[2,1024]{1,0:T(2,128)S(1)} %get-tuple-element.103), kind=kOutput, calls=%fused_computation.71 | convolution fusion | flops 551816192 | bytes 17833984 | tf_op jit(solution)/shard_map/while/body/eval_jaxpr/hqk,qhd->khd/dot_general | solution.py:45
  160.9 5.1 %fusion.87 = bf16[2,128,1024]{2,1,0:T(8,128)(2,1)S(1)} fusion(bf16[1024,2,128]{0,2,1:T(8,128)(2,1)S(1)} %bitcast.170, f32[2,1024,1024]{1,2,0:T(8,128)} %get-tuple-element.104, f32[2,1024]{1,0:T(2,128)S(1)} %get-tuple-element.103), kind=kOutput, calls=%fused_computation.65 | convolution fusion | flops 541327360 | bytes 9445376 | tf_op jit(solution)/shard_map/while/body/eval_jaxpr/hqk,qhd->khd/dot_general | solution.py:48
  166.0 90.1 %all-to-all-done.8 = bf16[16,64,6144]{2,1,0:T(8,128)(2,1)} async-done(((bf16[16,64,6144]{2,1,0:T(8,128)(2,1)}), bf16[16,64,6144]{2,1,0:T(8,128)(2,1)}, u32[]{:S(2)}, u32[]{:S(2)}) %all-to-all-start.8) | async-done | bytes 12582944 | tf_op jit(solution)/shard_map/all_to_all | solution.py:111
  256.0 17.1 %fusion.2 = bf16[6144,3,256]{0,2,1:T(8,128)(2,1)} fusion(bf16[1024,6144,1]{1,0,2:T(8,128)(2,1)} %bitcast.59, bf16[1,1024,1,256]{1,3,2,0:T(8,128)(2,1)S(1)} %bitcast.176, bf16[1,1024,1,256]{1,3,2,0:T(8,128)(2,1)S(1)} %bitcast.174, bf16[1,1024,1,256]{1,3,2,0:T(8,128)(2,1)S(1)} %bitcast.172), kind=kOutput, calls=%fused_computation.4 | convolution fusion | flops 9674686464 | bytes 23592960 | tf_op jit(solution)/shard_map/gsd,gstc->dtgc/dot_general | solution.py:132
  283.4 48.9 %all-to-all-start.3 = ((bf16[16,2,16384]{2,1,0:T(2,128)(2,1)}), bf16[16,2,16384]{2,1,0:T(2,128)(2,1)S(1)}, u32[]{:S(2)}, u32[]{:S(2)}) async-start(bf16[16,2,16384]{2,1,0:T(2,128)(2,1)} %reshape.812), calls=%async_computation.3 | async-start | bytes 2097152 | tf_op jit(solution)/shard_map/all_to_all | solution.py:151
  332.3 4.4 %fusion.63 = bf16[2048,1,256]{0,2,1:T(8,128)(2,1)} fusion(bf16[1024,256]{0,1:T(8,128)(2,1)} %bitcast.177, s32[1024]{0:T(1024)S(1)} %get-tuple-element.106, pred[1024]{0:T(1024)(128)(4,1)S(1)} %fusion.120), kind=kOutput, calls=%fused_computation.50 | convolution fusion | flops 1078460416 | bytes 1577984 | tf_op jit(solution)/shard_map/gsp,gsc->pgc/dot_general | solution.py:145
  343.3 6.8 %all-to-all-start.7 = ((bf16[16,2,16384]{2,1,0:T(2,128)(2,1)}), bf16[16,2,16384]{2,1,0:T(2,128)(2,1)S(1)}, u32[]{:S(2)}, u32[]{:S(2)}) async-start(bf16[16,2,16384]{2,1,0:T(2,128)(2,1)} %reshape.818), calls=%async_computation.7 | async-start | bytes 2097152 | tf_op jit(solution)/shard_map/all_to_all | solution.py:154
  361.1 7.2 %all-to-all-start.6 = ((bf16[16,2,16384]{2,1,0:T(2,128)(2,1)}), bf16[16,2,16384]{2,1,0:T(2,128)(2,1)}, u32[]{:S(2)}, u32[]{:S(2)}) async-start(bf16[16,2,16384]{2,1,0:T(2,128)(2,1)} %reshape.816), calls=%async_computation.6 | async-start | bytes 2097152 | tf_op jit(solution)/shard_map/all_to_all | solution.py:153
  379.4 7.6 %all-to-all-start.5 = ((bf16[16,2,16384]{2,1,0:T(2,128)(2,1)}), bf16[16,2,16384]{2,1,0:T(2,128)(2,1)}, u32[]{:S(2)}, u32[]{:S(2)}) async-start(bf16[16,2,16384]{2,1,0:T(2,128)(2,1)} %reshape.814), calls=%async_computation.5 | async-start | bytes 2097152 | tf_op jit(solution)/shard_map/all_to_all | solution.py:152
  403.0 5.8 %reshape.817 = bf16[2048,1,256]{2,1,0:T(2,128)(2,1)} reshape(bf16[16,2,16384]{2,1,0:T(2,128)(2,1)} %all-to-all-done.6) | data formatting | bytes 2097152
  414.1 5.8 %reshape.815 = bf16[2048,1,256]{2,1,0:T(2,128)(2,1)} reshape(bf16[16,2,16384]{2,1,0:T(2,128)(2,1)} %all-to-all-done.5) | data formatting | bytes 2097152
  (87 shorter events, 103.3 us)
Async XLA Ops:
  7.2 71.2 %copy-start = (bf16[128,6144]{1,0:T(8,128)(2,1)S(1)}, bf16[128,6144]{1,0:T(8,128)(2,1)}, u32[]{:S(2)}) copy-start(bf16[128,6144]{1,0:T(8,128)(2,1)} %param.8) | copy-start | bytes 4718596
  7.2 54.4 %copy-start.4 = (s32[16]{0:T(128)S(1)}, s32[16]{0:T(128)}, u32[]{:S(2)}) copy-start(s32[16]{0:T(128)} %param.14) | copy-start | bytes 196
  9.6 23.5 %all-to-all-start.1 = ((bf16[128,16,256]{0,2,1:T(8,128)(2,1)}), bf16[128,16,256]{0,2,1:T(8,128)(2,1)S(1)}, u32[]{:S(2)}, u32[]{:S(2)}) async-start(bf16[128,16,256]{0,2,1:T(8,128)(2,1)} %bitcast.158), calls=%async_computation.1 | async-start | bytes 2097152 | tf_op jit(solution)/shard_map/all_to_all | solution.py:106
  33.0 19.8 %all-to-all-start.2 = ((bf16[128,16,256]{0,2,1:T(8,128)(2,1)}), bf16[128,16,256]{0,2,1:T(8,128)(2,1)}, u32[]{:S(2)}, u32[]{:S(2)}) async-start(bf16[128,16,256]{0,2,1:T(8,128)(2,1)} %bitcast.157), calls=%async_computation.2 | async-start | bytes 2097152 | tf_op jit(solution)/shard_map/all_to_all | solution.py:107
  52.8 19.2 %all-to-all-start = ((bf16[128,16,256]{0,2,1:T(8,128)(2,1)}), bf16[128,16,256]{0,2,1:T(8,128)(2,1)}, u32[]{:S(2)}, u32[]{:S(2)}) async-start(bf16[128,16,256]{0,2,1:T(8,128)(2,1)} %bitcast.156), calls=%async_computation | async-start | bytes 2097152 | tf_op jit(solution)/shard_map/all_to_all | solution.py:108
  72.1 19.0 %all-to-all-start.4 = ((bf16[128,16,256]{0,2,1:T(8,128)(2,1)}), bf16[128,16,256]{0,2,1:T(8,128)(2,1)}, u32[]{:S(2)}, u32[]{:S(2)}) async-start(bf16[128,16,256]{0,2,1:T(8,128)(2,1)} %bitcast.155), calls=%async_computation.4 | async-start | bytes 2097152 | tf_op jit(solution)/shard_map/all_to_all | solution.py:109
  84.8 14.6 %copy-start.5 = (s32[16]{0:T(128)S(1)}, s32[16]{0:T(128)}, u32[]{:S(2)}) copy-start(s32[16]{0:T(128)} %param.15) | copy-start | bytes 196
  84.8 15.9 %copy-start.6 = (s32[1,16]{1,0:T(1,128)S(1)}, s32[1,16]{1,0:T(1,128)}, u32[]{:S(2)}) copy-start(s32[1,16]{1,0:T(1,128)} %param.13) | copy-start | bytes 196
  91.1 164.9 %all-to-all-start.8 = ((bf16[16,64,6144]{2,1,0:T(8,128)(2,1)}), bf16[16,64,6144]{2,1,0:T(8,128)(2,1)}, u32[]{:S(2)}, u32[]{:S(2)}) async-start(bf16[16,64,6144]{2,1,0:T(8,128)(2,1)} %convolution_convert_fusion), calls=%async_computation.8 | async-start | bytes 25165824 | tf_op jit(solution)/shard_map/all_to_all | solution.py:111
  97.9 327.3 %reduce-scatter.2.cloned.1.call-start = ((), (), s32[]{:S(2)}) async-start(), calls=%async_computation.10 | async-start | bytes 10616832 | tf_op jit(solution)/shard_map/reduce_scatter | solution.py:133
  111.1 7.9 %copy-start.2 = (bf16[16,128,1,256]{3,1,0,2:T(8,128)(2,1)S(1)}, bf16[16,128,1,256]{3,1,0,2:T(8,128)(2,1)}, u32[]{:S(2)}) copy-start(bf16[16,128,1,256]{3,1,0,2:T(8,128)(2,1)} %copy.136) | copy-start | bytes 3145732
  115.3 14.1 %copy-start.10 = (bf16[1024,256]{0,1:T(8,128)(2,1)}, bf16[1024,256]{0,1:T(8,128)(2,1)S(1)}, u32[]{:S(2)}) copy-start(bf16[1024,256]{0,1:T(8,128)(2,1)S(1)} %fusion.93) | copy-start | bytes 1572868
  115.3 6.6 %copy-start.3 = (bf16[16,128,1,256]{3,1,0,2:T(8,128)(2,1)S(1)}, bf16[16,128,1,256]{3,1,0,2:T(8,128)(2,1)}, u32[]{:S(2)}) copy-start(bf16[16,128,1,256]{3,1,0,2:T(8,128)(2,1)} %copy.147) | copy-start | bytes 3145732
  121.9 7.5 %copy-start.12 = (bf16[1024,256]{0,1:T(8,128)(2,1)S(1)}, bf16[1024,256]{0,1:T(8,128)(2,1)}, u32[]{:S(2)}) copy-start(bf16[1024,256]{0,1:T(8,128)(2,1)} %fusion.96) | copy-start | bytes 1572868
  134.8 13.6 %copy-start.11 = (bf16[1024,256]{0,1:T(8,128)(2,1)S(1)}, bf16[1024,256]{0,1:T(8,128)(2,1)}, u32[]{:S(2)}) copy-start(bf16[1024,256]{0,1:T(8,128)(2,1)} %copy-done.10) | copy-start | bytes 1572868
  160.8 95.2 %copy-start.7 = (bf16[2,128,1024]{2,1,0:T(8,128)(2,1)}, bf16[2,128,1024]{2,1,0:T(8,128)(2,1)S(1)}, u32[]{:S(2)}) copy-start(bf16[2,128,1024]{2,1,0:T(8,128)(2,1)S(1)} %fusion.105) | copy-start | bytes 1572868
  166.0 107.2 %copy-start.9 = (bf16[2,128,1024]{2,1,0:T(8,128)(2,1)}, bf16[2,128,1024]{2,1,0:T(8,128)(2,1)S(1)}, u32[]{:S(2)}) copy-start(bf16[2,128,1024]{2,1,0:T(8,128)(2,1)S(1)} %fusion.87) | copy-start | bytes 1572868
  283.4 59.9 %all-to-all-start.3 = ((bf16[16,2,16384]{2,1,0:T(2,128)(2,1)}), bf16[16,2,16384]{2,1,0:T(2,128)(2,1)S(1)}, u32[]{:S(2)}, u32[]{:S(2)}) async-start(bf16[16,2,16384]{2,1,0:T(2,128)(2,1)} %reshape.812), calls=%async_computation.3 | async-start | bytes 2097152 | tf_op jit(solution)/shard_map/all_to_all | solution.py:151
  332.3 17.7 %copy-start.8 = (bf16[2,128,1024]{2,1,0:T(8,128)(2,1)S(1)}, bf16[2,128,1024]{2,1,0:T(8,128)(2,1)}, u32[]{:S(2)}) copy-start(bf16[2,128,1024]{2,1,0:T(8,128)(2,1)} %copy-done.7) | copy-start | bytes 1572868
  343.3 17.8 %all-to-all-start.7 = ((bf16[16,2,16384]{2,1,0:T(2,128)(2,1)}), bf16[16,2,16384]{2,1,0:T(2,128)(2,1)S(1)}, u32[]{:S(2)}, u32[]{:S(2)}) async-start(bf16[16,2,16384]{2,1,0:T(2,128)(2,1)} %reshape.818), calls=%async_computation.7 | async-start | bytes 2097152 | tf_op jit(solution)/shard_map/all_to_all | solution.py:154
  361.1 18.3 %all-to-all-start.6 = ((bf16[16,2,16384]{2,1,0:T(2,128)(2,1)}), bf16[16,2,16384]{2,1,0:T(2,128)(2,1)}, u32[]{:S(2)}, u32[]{:S(2)}) async-start(bf16[16,2,16384]{2,1,0:T(2,128)(2,1)} %reshape.816), calls=%async_computation.6 | async-start | bytes 2097152 | tf_op jit(solution)/shard_map/all_to_all | solution.py:153
  379.4 34.7 %all-to-all-start.5 = ((bf16[16,2,16384]{2,1,0:T(2,128)(2,1)}), bf16[16,2,16384]{2,1,0:T(2,128)(2,1)}, u32[]{:S(2)}, u32[]{:S(2)}) async-start(bf16[16,2,16384]{2,1,0:T(2,128)(2,1)} %reshape.814), calls=%async_computation.5 | async-start | bytes 2097152 | tf_op jit(solution)/shard_map/all_to_all | solution.py:152
  410.5 17.4 %copy-start.1 = (bf16[128,6144]{1,0:T(8,128)(2,1)S(1)}, bf16[128,6144]{1,0:T(8,128)(2,1)}, u32[]{:S(2)}) copy-start(bf16[128,6144]{1,0:T(8,128)(2,1)} %param.8) | copy-start | bytes 4718596
Sparse Core Ops, SparseCore 0:
  273.3 100.1 reduce-scatter.1
where the time goes:
time: 440 us; the launch traced here: 435 us
  waiting for transfers between devices  131 us (30%)
  starting transfers between devices  105 us (24%)
  matrix products  95.5 us (22%)
  local copies, waits for them, and re-layouts  73.2 us (17%)
  between operations  16.2 us (4%)
  other arithmetic  14.1 us (3%)
    all_to_all x1, waiting for transfers between devices, on_device(): lax.all_to_all(input_taken, 'ctx', split_axis=0, concat_axis=1, tiled=True)  90.1 us
    unnamed x51, local copies, waits for them, and re-layouts  59.6 us
    all_to_all x1, starting transfers between devices, on_device(): lax.all_to_all(spread[0], 'ctx', split_axis=0, concat_axis=1, tiled=True)  48.9 us
    dot_general x1, matrix products, on_device(): jnp.einsum('gsd,gstc->dtgc', input_slots, stacked, preferred_element_type...  17.1 us
    dot_general x4, matrix products, on_device(): jnp.einsum('gsp,pgc->gsc', owner_select, tensor, preferred_element_type=j...  13.7 us
    dot_general x1, matrix products, attend(): jnp.einsum('hqk,khd->qhd', dscore, key_heads, preferred_element_type=jnp....  13.6 us
    dot_general x4, matrix products, on_device(): jnp.einsum('gsp,gsc->pgc', owner_select, tensor, preferred_element_type=j...  13.3 us
    all_to_all x1, waiting for transfers between devices, on_device(): lax.all_to_all(shaped[0], 'ctx', split_axis=1, concat_axis=0, tiled=True)  12.8 us
  transfers between devices with their start and end apart: 10, of which 7 were waited for; matrix products, arithmetic and copies ran while one was open for 37% of the time, Pallas kernels for 0%

commit v1 on v0

v1 whole, which is shorter than its diff:
```python
import functools
import math

import jax
import jax.numpy as jnp
from jax import lax
from jax.experimental import pallas as pl
from jax.experimental.pallas import tpu as pltpu
from jax.sharding import PartitionSpec as P

MESH = pl.DeviceIdType.MESH
HS = 128
SIDE = 4
CTX = 16
ROWS = 128
HALF = 64
SLOTS = 1024
GW = 256
D = 6144
BLOCK = 768
CHUNKS = 4
BQ = 256
BF = jnp.bfloat16
F32 = jnp.float32
OFFSETS = (
    (0, 1), (1, 0), (0, 3), (3, 0), (1, 1), (3, 3), (1, 3), (3, 1),
    (0, 2), (2, 0), (1, 2), (2, 1), (3, 2), (2, 3), (2, 2),
)


def nt(a, b):
    return lax.dot_general(a, b, (((1,), (1,)), ((), ())), preferred_element_type=F32)


def nn(a, b):
    return jnp.dot(a, b, preferred_element_type=F32)


def slot_ids(shape, dim, parity, group, lengths, rate, seg_len):
    pos = 2 * lax.broadcasted_iota(jnp.int32, shape, dim) + parity
    doc = jnp.zeros(shape, jnp.int32)
    end = jnp.int32(0)
    for d in range(16):
        end = end + lengths[0, d]
        doc = doc + (pos >= end).astype(jnp.int32)
    seg = jnp.zeros(shape, jnp.int32)
    for m in range(1, 8):
        seg = seg + (pos >= m * seg_len).astype(jnp.int32)
    usable = ((pos - group) & (rate - 1)) == 0
    return doc * 8 + seg, usable


def kernel(
    x_hbm, q_hbm, k_hbm, v_hbm, g_hbm, lengths, rates, segs,
    back, wsum,
    x_in, t_in, sq, rq, xo, xg, yb, gt, idk_ref, idq_ref, use_ref, kt, vt, gk_acc, gv_acc,
    pb, sib, rbuf, rel, rx,
    load_sem, loc_sem, bar_free, a_ss, a_rs, b_ss, b_rs, x_ss, x_rs, w_ss, w_rs,
):
    del bar_free
    dp = lax.axis_index("dp")
    me = lax.axis_index("ctx")
    xx, core = dp // 2, dp % 2
    yy, zz = me // SIDE, me % SIDE
    parity = zz % 2

    def at(dy, dz):
        return ((yy + dy) % SIDE) * SIDE + (zz + dz) % SIDE

    def at_x(dx):
        return ((xx + dx) % 4) * 2 + core

    loads = [
        pltpu.make_async_copy(src, t_in.at[i], load_sem.at[i])
        for i, src in enumerate((q_hbm, k_hbm, v_hbm, g_hbm))
    ]
    loads.append(pltpu.make_async_copy(x_hbm, x_in, load_sem.at[4]))
    for load in loads:
        load.start()

    barrier = pltpu.get_barrier_semaphore()
    peers = [(dp, at(dy, dz)) for dy, dz in OFFSETS]
    peers += [(xx * 2 + 1 - core, me), (at_x(1), me), (at_x(3), me)]
    for peer in peers:
        pl.semaphore_signal(barrier, inc=1, device_id=peer, device_id_type=MESH)
    pl.semaphore_wait(barrier, len(peers))

    pending = []

    def send(src, dst, ss, rs, peer):
        copy = pltpu.make_async_remote_copy(
            src_ref=src, dst_ref=dst, send_sem=ss, recv_sem=rs, device_id=peer, device_id_type=MESH
        )
        copy.start()
        return copy

    for load in loads[:4]:
        load.wait()
    row = lax.broadcasted_iota(jnp.int32, (HALF, ROWS), 0)
    col = lax.broadcasted_iota(jnp.int32, (HALF, ROWS), 1)
    picks = [(col == 2 * row + par).astype(F32).astype(BF) for par in range(2)]

    def gather_group(pair, carry):
        for par in range(2):
            group = 2 * pair + par
            cols = pl.ds(pl.multiple_of(group * GW, GW), GW)
            for t in range(4):
                sq[group, t] = nn(picks[par], t_in[t, :, cols]).astype(BF)
        return carry

    lax.fori_loop(0, CTX // 2, gather_group, 0)
    own_q = pltpu.make_async_copy(sq.at[me], rq.at[me], loc_sem.at[0])
    own_q.start()
    out_q = [
        send(sq.at[at(dy, dz)], rq.at[me], a_ss.at[i], a_rs.at[i], (dp, at(dy, dz)))
        for i, (dy, dz) in enumerate(OFFSETS)
    ]

    loads[4].wait()
    row2 = lax.broadcasted_iota(jnp.int32, (ROWS, ROWS), 0)
    col2 = lax.broadcasted_iota(jnp.int32, (ROWS, ROWS), 1)
    wanted = jnp.where(row2 < HALF, 2 * row2 + parity, 2 * (row2 - HALF) + 1 - parity)
    permute = (col2 == wanted).astype(F32).astype(BF)
    targets = [(xx + 2) % 4, (xx + 1) % 4, (xx + 3) % 4, xx]
    stage = [dict() for _ in range(CHUNKS)]

    def xsend(k, name, i, src, dst, dy, dz):
        stage[k][name] = send(src, dst, x_ss.at[k, i], x_rs.at[k, i], (dp, at(dy, dz)))

    def first(k):
        base = targets[k] * (2 * BLOCK)
        for part in range(2):
            for n in range(3):
                cols = pl.ds(pl.multiple_of(base + part * BLOCK + n * 256, 256), 256)
                here = slice(n * 256, (n + 1) * 256)
                both = nn(permute, x_in[:, cols]).astype(BF)
                if part == 0:
                    xg[k, 0, yy, zz, :, here] = both[:HALF]
                    xo[k, :, here] = both[HALF:]
                else:
                    yb[k, 0, yy, :, here] = both[:HALF]
                    yb[k, 1, yy, :, here] = both[HALF:]
        home = xg.at[k, 0, yy, zz]
        xsend(k, "a1p", 0, xo.at[k], home, 0, 1)
        xsend(k, "a1m", 1, xo.at[k], home, 0, 3)
        xsend(k, "b1p", 3, yb.at[k, :, yy], yb.at[k, :, yy], 1, 0)
        xsend(k, "b1m", 4, yb.at[k, :, yy], yb.at[k, :, yy], 3, 0)
        xsend(k, "a12", 2, home, home, 0, 2)

    def second(k):
        stage[k]["a1p"].wait_recv()
        stage[k]["a1m"].wait_recv()
        stage[k]["a12"].wait_recv()
        mine = xg.at[k, 0, yy]
        xsend(k, "a2p", 5, mine, mine, 1, 0)
        xsend(k, "a2m", 6, mine, mine, 3, 0)
        stage[k]["b1p"].wait_recv()
        below = yb.at[k, 0, (yy + 3) % SIDE]
        xsend(k, "b2p", 7, below, below, 1, 0)
        stage[k]["b1m"].wait_recv()
        above = yb.at[k, 1, (yy + 1) % SIDE]
        xsend(k, "b2m", 8, above, above, 3, 0)

    def third(k):
        stage[k]["b2p"].wait_recv()
        stage[k]["b2m"].wait_recv()
        there = xg.at[k, 1, :, zz]
        xsend(k, "b3p", 9, yb.at[k, 1], there, 0, 1)
        xsend(k, "b3m", 10, yb.at[k, 1], there, 0, 3)
        xsend(k, "b32", 11, yb.at[k, 0], there, 0, 2)
        local = pltpu.make_async_copy(yb.at[k, 0], there, loc_sem.at[1 + k])
        local.start()
        stage[k]["local"] = local
        stage[k]["a2p"].wait_recv()
        below = xg.at[k, 0, (yy + 3) % SIDE, 0:2]
        xsend(k, "a3p", 12, below, below, 1, 0)
        stage[k]["a2m"].wait_recv()
        above = xg.at[k, 0, (yy + 1) % SIDE, 2:4]
        xsend(k, "a3m", 13, above, above, 3, 0)

    def arrived(k):
        stage[k].pop("local").wait()
        for name in ("a3p", "a3m", "b3p", "b3m", "b32"):
            stage[k][name].wait_recv()

    for k in range(CHUNKS):
        first(k)

    rate, seg_len = rates[me], segs[me]
    ids, usable = slot_ids((SLOTS, 1), 0, parity, me, lengths, rate, seg_len)
    idk_ref[...] = jnp.where(usable, ids, -1)
    ids, usable = slot_ids((1, SLOTS), 1, parity, me, lengths, rate, seg_len)
    idq_ref[...] = jnp.where(usable, ids, -2)
    use_ref[...] = usable.astype(F32)

    second(0)
    second(1)
    own_q.wait()
    for copy in out_q:
        copy.wait_recv()
    for copy in out_q:
        copy.wait_send()

    scale = 1.0 / math.sqrt(HS)
    log2e = 1.4426950408889634

    def heads(h, t, count):
        return rq[0:count, t, :, h * HS:(h + 1) * HS].reshape(count * HALF, HS)

    def attend(h, i):
        count = (i + 1) * (BQ // HALF)
        w = (i + 1) * BQ
        mine = slice(i * (BQ // HALF), (i + 1) * (BQ // HALF))
        cols = slice(h * HS, (h + 1) * HS)
        q = rq[mine, 0, :, cols].reshape(BQ, HS)
        g = rq[mine, 3, :, cols].reshape(BQ, HS)
        queries = slice(i * BQ, (i + 1) * BQ)
        idq = idq_ref[:, queries]
        allowed = (idk_ref[0:w] == idq) & (
            lax.broadcasted_iota(jnp.int32, (w, BQ), 0)
            <= lax.broadcasted_iota(jnp.int32, (w, BQ), 1) + i * BQ
        )
        s = jnp.where(allowed, nt(heads(h, 1, count), q) * (scale * log2e), -1e30)
        e = jnp.exp2(s - jnp.max(s, axis=0, keepdims=True))
        p = e * (use_ref[:, queries] / jnp.sum(e, axis=0, keepdims=True))
        weights = p.astype(BF)
        dprob = nt(heads(h, 2, count), g)
        delta = jnp.sum(p * dprob, axis=0, keepdims=True)
        ds = (p * (dprob - delta) * scale).astype(BF)
        out_t = nn(vt[:, 0:w], weights).astype(BF)
        gq_t = nn(kt[:, 0:w], ds).astype(BF)
        gt[h * HS:(h + 1) * HS, queries] = gq_t
        sq[mine, 0, :, cols] = out_t.T.reshape(BQ // HALF, HALF, HS)
        sq[mine, 1, :, cols] = gq_t.T.reshape(BQ // HALF, HALF, HS)
        gk, gv = nn(ds, q), nn(weights, g)
        if i == SLOTS // BQ - 1:
            gk_acc[...] = gk
            gv_acc[...] = gv
        else:
            gk_acc[0:w] += gk
            gv_acc[0:w] += gv

    def begin_head(h):
        kt[...] = heads(h, 1, CTX).T
        vt[...] = heads(h, 2, CTX).T

    def end_head(h):
        cols = slice(h * HS, (h + 1) * HS)
        for t, acc in ((2, gk_acc), (3, gv_acc)):
            value = acc[...].astype(BF)
            sq[:, t, :, cols] = value.reshape(CTX, HALF, HS)
            gt[(t - 1) * GW + h * HS:(t - 1) * GW + (h + 1) * HS, :] = value.T

    between = {(0, 3): (second, 2), (0, 1): (second, 3), (1, 3): (third, 0), (1, 1): (third, 1)}
    for h in range(2):
        begin_head(h)
        for i in reversed(range(SLOTS // BQ)):
            attend(h, i)
            if (h, i) in between:
                step, k = between[(h, i)]
                step(k)
        end_head(h)

    own_back = pltpu.make_async_copy(sq.at[me], back.at[me], loc_sem.at[0])
    own_back.start()
    out_back = [
        send(sq.at[at(dy, dz)], back.at[me], b_ss.at[i], b_rs.at[i], (dp, at(dy, dz)))
        for i, (dy, dz) in enumerate(OFFSETS)
    ]

    third(2)
    sibling = (xx * 2 + 1 - core, me)
    sums = {}

    def product(k):
        if k >= 2:
            sums["sib", k - 2].wait_send()

        def tile(n, carry):
            part = n // 3
            cols = pl.ds(pl.multiple_of((n % 3) * 256, 256), 256)
            rows = xg[k, part, :, :, :, cols].reshape(SLOTS, 256)
            pb[k % 2, part, :, cols] = nn(gt[...], rows).astype(BF)
            return carry

        lax.fori_loop(0, 6, tile, 0)
        sums["sib", k] = send(
            pb.at[k % 2, 1 - core], sib.at[k], w_ss.at[k], w_rs.at[k], sibling
        )

    def pair(k, lo, hi):
        return pb[k % 2, core, lo:hi].astype(F32) + sib[k, lo:hi].astype(F32)

    def reduce(k):
        sums["sib", k].wait_recv()
        mid = BLOCK // 2
        if k == 0:
            rbuf[0, 0:mid] = pair(k, 0, mid).astype(BF)
            sums["ra"] = send(rbuf.at[0, 0:mid], rel.at[0], w_ss.at[4], w_rs.at[4], (at_x(3), me))
            rbuf[0, mid:] = pair(k, mid, BLOCK).astype(BF)
            sums["rb"] = send(rbuf.at[0, mid:], rel.at[1], w_ss.at[5], w_rs.at[5], (at_x(1), me))
        if k == 1:
            rbuf[1, 0:mid] = pair(k, 0, mid).astype(BF)
            sums["rb"].wait_recv()
            rbuf[1, mid:] = (pair(k, mid, BLOCK) + rel[1].astype(F32)).astype(BF)
            sums["xp"] = send(rbuf.at[1], rx.at[0], w_ss.at[6], w_rs.at[6], (at_x(1), me))
        if k == 2:
            sums["ra"].wait_recv()
            rbuf[2, 0:mid] = (pair(k, 0, mid) + rel[0].astype(F32)).astype(BF)
            rbuf[2, mid:] = pair(k, mid, BLOCK).astype(BF)
            sums["xm"] = send(rbuf.at[2], rx.at[1], w_ss.at[7], w_rs.at[7], (at_x(3), me))
        if k == 3:
            sums["xp"].wait_recv()
            sums["xm"].wait_recv()
            total = pair(k, 0, BLOCK) + rx[0].astype(F32) + rx[1].astype(F32)
            wsum[...] = total * (1.0 / 128.0)

    arrived(0)
    product(0)
    third(3)
    reduce(0)
    for k in range(1, CHUNKS):
        arrived(k)
        product(k)
        reduce(k)

    own_back.wait()
    for copy in out_back:
        copy.wait_recv()
        copy.wait_send()
    for k in range(CHUNKS):
        for copy in stage[k].values():
            copy.wait_send()
    for name in (("sib", 2), ("sib", 3), "ra", "rb", "xp", "xm"):
        sums[name].wait_send()


def finish_kernel(back, wsum, out, gq, gk, gv, weight):
    row = lax.broadcasted_iota(jnp.int32, (ROWS, HALF), 0)
    col = lax.broadcasted_iota(jnp.int32, (ROWS, HALF), 1)
    for group in range(8):
        spread = (row == 2 * col + group % 2).astype(F32).astype(BF)
        for t, ref in enumerate((out, gq, gk, gv)):
            ref[:, group * GW:(group + 1) * GW] = nn(spread, back[group, t]).astype(BF)
    for j in range(3):
        weight[j] = wsum[j * GW:(j + 1) * GW, :].T


def on_device(
    layer_input, query_rows, key_rows, value_rows, out_grad, doc_lengths, dilations, seg_lengths
):
    hbm = pl.BlockSpec(memory_space=pl.ANY)
    smem = pl.BlockSpec(memory_space=pltpu.SMEM)
    vmem = pl.BlockSpec(memory_space=pltpu.VMEM)
    dma = pltpu.SemaphoreType.DMA
    back, wsum = pl.pallas_call(
        kernel,
        out_shape=(
            jax.ShapeDtypeStruct((CTX, 4, HALF, GW), BF),
            jax.ShapeDtypeStruct((BLOCK, BLOCK), F32),
        ),
        in_specs=[hbm] * 5 + [smem] * 3,
        out_specs=(hbm, vmem),
        scratch_shapes=[
            pltpu.VMEM((ROWS, D), BF),
            pltpu.VMEM((4, ROWS, 4096), BF),
            pltpu.VMEM((CTX, 4, HALF, GW), BF),
            pltpu.VMEM((CTX, 4, HALF, GW), BF),
            pltpu.VMEM((CHUNKS, HALF, BLOCK), BF),
            pltpu.VMEM((CHUNKS, 2, SIDE, SIDE, HALF, BLOCK), BF),
            pltpu.VMEM((CHUNKS, 2, SIDE, HALF, BLOCK), BF),
            pltpu.VMEM((3 * GW, SLOTS), BF),
            pltpu.VMEM((SLOTS, 1), jnp.int32),
            pltpu.VMEM((1, SLOTS), jnp.int32),
            pltpu.VMEM((1, SLOTS), F32),
            pltpu.VMEM((HS, SLOTS), BF),
            pltpu.VMEM((HS, SLOTS), BF),
            pltpu.VMEM((SLOTS, HS), F32),
            pltpu.VMEM((SLOTS, HS), F32),
            pltpu.VMEM((2, 2, BLOCK, BLOCK), BF),
            pltpu.VMEM((CHUNKS, BLOCK, BLOCK), BF),
            pltpu.VMEM((3, BLOCK, BLOCK), BF),
            pltpu.VMEM((2, BLOCK // 2, BLOCK), BF),
            pltpu.VMEM((2, BLOCK, BLOCK), BF),
            dma((5,)),
            dma((5,)),
            pltpu.SemaphoreType.REGULAR,
            dma((15,)),
            dma((15,)),
            dma((15,)),
            dma((15,)),
            dma((CHUNKS, 14)),
            dma((CHUNKS, 14)),
            dma((8,)),
            dma((8,)),
        ],
        compiler_params=pltpu.CompilerParams(
            collective_id=0, has_side_effects=True, vmem_limit_bytes=60 * 2**20
        ),
    )(layer_input, query_rows, key_rows, value_rows, out_grad, doc_lengths, dilations, seg_lengths)
    wide = jax.ShapeDtypeStruct((ROWS, 4096), BF)
    out, gq, gk, gv, weight = pl.pallas_call(
        finish_kernel,
        grid=(2,),
        out_shape=(wide, wide, wide, wide, jax.ShapeDtypeStruct((3, BLOCK, GW), F32)),
        in_specs=[
            pl.BlockSpec((8, 4, HALF, GW), lambda i: (i, 0, 0, 0)),
            pl.BlockSpec((BLOCK, BLOCK // 2), lambda i: (0, i)),
        ],
        out_specs=[pl.BlockSpec((ROWS, 2048), lambda i: (0, i))] * 4
        + [pl.BlockSpec((3, BLOCK // 2, GW), lambda i: (0, i, 0))],
        compiler_params=pltpu.CompilerParams(vmem_limit_bytes=40 * 2**20),
    )(back, wsum)
    return out, gq, gk, gv, jnp.transpose(weight, (1, 0, 2))


def solution(mesh):
    rows = P(("dp", "ctx"), None)
    return jax.shard_map(
        on_device,
        mesh=mesh,
        in_specs=(rows, rows, rows, rows, rows, P("dp", None), P(), P()),
        out_specs=(rows, rows, rows, rows, P("dp", None, "ctx")),
        check_vma=False,
    )
```

time: 440 us -> 183 us (0.42)
  the two profiles are of different devices: /device:TPU:8 before, /device:TPU:1 now
where the time goes in v1:
time: 183 us
  Pallas kernels  179 us (98%)
  local copies, waits for them, and re-layouts  3.25 us (2%)
    pallas_call x1, Pallas kernels, on_device(): pl.pallas_call(kernel, out_shape=(jax.ShapeDtypeStruct((CTX, 4, HALF, GW)...  175 us

profile of v1, /device:TPU:1, one launch (start us, length us, event | category | flops | bytes accessed | tf_op | source)
XLA Modules:
  0.0 183.0 jit_solution(3870165685623771068)
XLA Ops:
  0.6 175.5 %shard_map.119 = (bf16[16,4,64,256]{3,2,1,0:T(8,128)(2,1)}, f32[768,768]{1,0:T(8,128)}) custom-call(bf16[128,6144]{1,0:T(8,128)(2,1)} %x_hbm.1, bf16[128,4096]{1,0:T(8,128)(2,1)} %q_hbm.1, bf16[128,4096]{1,0:T(8,128)(2,1)} %k_hbm.1, bf16[128,4096]{1,0:T(8,128)(2,1)} %v_hbm.1, bf16[128,4096]{1,0:T(8,128)(2,1)} %g_hbm.1, s32[1,16]{1,0:T(1,128)} %lengths.1, ...), custom_call_target="tpu_custom_call" | custom-call | tf_op jit(solution)/shard_map/pallas_call | solution.py:356
  176.1 0.0 copy-start
  176.1 1.7 copy-done
  177.8 0.0 copy-start.1
  177.8 1.6 copy-done.1
  179.4 3.6 %shard_map.120 = (bf16[128,4096]{1,0:T(8,128)(2,1)}, bf16[128,4096]{1,0:T(8,128)(2,1)}, bf16[128,4096]{1,0:T(8,128)(2,1)}, bf16[128,4096]{1,0:T(8,128)(2,1)}, f32[3,768,256]{2,1,0:T(8,128)}) custom-call(bf16[16,4,64,256]{3,2,1,0:T(8,128)(2,1)S(1)} %copy-done.1, f32[768,768]{1,0:T(8,128)S(1)} %copy-done), custom_call_target="tpu_custom_call" | custom-call | tf_op jit(solution)/shard_map/pallas_call | solution.py:402
Async XLA Ops:
  176.1 1.7 copy-start
  177.8 1.6 copy-start.1

commit v2 on v1

v2 whole, which is shorter than its diff:
```python
import functools
import math

import jax
import jax.numpy as jnp
from jax import lax
from jax.experimental import pallas as pl
from jax.experimental.pallas import tpu as pltpu
from jax.sharding import PartitionSpec as P

MESH = pl.DeviceIdType.MESH
HS = 128
SIDE = 4
CTX = 16
ROWS = 128
HALF = 64
SLOTS = 1024
GW = 256
D = 6144
BLOCK = 768
CHUNKS = 4
TILES = 3
UNITS = 6
BQ = 256
BF = jnp.bfloat16
F32 = jnp.float32
SPREAD = (2, 1, 1, 1)


def nt(a, b):
    return lax.dot_general(a, b, (((1,), (1,)), ((), ())), preferred_element_type=F32)


def nn(a, b):
    return jnp.dot(a, b, preferred_element_type=F32)


def slot_ids(shape, dim, parity, group, lengths, rate, seg_len):
    pos = 2 * lax.broadcasted_iota(jnp.int32, shape, dim) + parity
    doc = jnp.zeros(shape, jnp.int32)
    end = jnp.zeros((1, 1), jnp.int32)
    for d in range(16):
        end = end + lengths[:, d:d + 1]
        doc = doc + (pos >= end).astype(jnp.int32)
    seg = jnp.zeros(shape, jnp.int32)
    for m in range(1, 8):
        seg = seg + (pos >= m * seg_len).astype(jnp.int32)
    usable = ((pos - group) & (rate - 1)) == 0
    return doc * 8 + seg, usable


def kernel(
    x_hbm, q_hbm, k_hbm, v_hbm, g_hbm, lengths, rates, segs,
    back, wsum,
    x_in, t_in, len_ref, sq, rq, xs, xg, yb, gt, idk_ref, idq_ref, use_ref, kt, vt, gk_acc, gv_acc,
    r_far, rel, near, rx, fin, ex, ex_in,
    load_sem, loc_sem, l_ss, l_rs, a_ss, a_rs, b_ss, b_rs, x_ss, x_rs, w_ss, w_rs,
):
    dp = lax.axis_index("dp")
    me = lax.axis_index("ctx")
    xx, core = dp // 2, dp % 2
    yy, zz = me // SIDE, me % SIDE
    half, tau = yy // 2, yy % 2
    parity = zz % 2
    group = (half * 2 + core) * SIDE + zz
    at_home = core == tau

    def dev(which, dy, dz):
        return (xx * 2 + which, ((yy + dy) % SIDE) * SIDE + (zz + dz) % SIDE)

    def dev_x(dx):
        return (((xx + dx) % 4) * 2 + core, me)

    sibling = dev(1 - core, 0, 0)

    loads = [
        pltpu.make_async_copy(src, t_in.at[i], load_sem.at[i])
        for i, src in enumerate((q_hbm, k_hbm, v_hbm, g_hbm))
    ]
    loads.append(pltpu.make_async_copy(x_hbm, x_in, load_sem.at[4]))
    for load in loads:
        load.start()
    len_ref[0, 0:1, 0:16] = lengths[...]

    barrier = pltpu.get_barrier_semaphore()
    peers = [
        dev((core + dc) % 2, dy, dz)
        for dc in range(2) for dy in range(SIDE) for dz in range(SIDE) if dc or dy or dz
    ]
    peers += [dev_x(1), dev_x(3)]
    for peer in peers:
        pl.semaphore_signal(barrier, inc=1, device_id=peer, device_id_type=MESH)
    pl.semaphore_wait(barrier, len(peers))

    sent = []

    def send(src, dst, ss, rs, peer):
        copy = pltpu.make_async_remote_copy(
            src_ref=src, dst_ref=dst, send_sem=ss, recv_sem=rs, device_id=peer, device_id_type=MESH
        )
        copy.start()
        sent.append(copy)
        return copy

    def send_or_keep(keep, src, dst, ss, rs, peer):
        copy = pltpu.make_async_remote_copy(
            src_ref=src, dst_ref=dst, send_sem=ss, recv_sem=rs, device_id=peer, device_id_type=MESH
        )

        @pl.when(keep)
        def _():
            pltpu.make_async_copy(src, dst, rs).start()

        @pl.when(jnp.logical_not(keep))
        def _():
            copy.start()

        return copy

    def wait_in(dst, rs):
        pltpu.make_async_copy(dst, dst, rs).wait()

    lens = send(len_ref.at[0], len_ref.at[1], l_ss.at[0], l_rs.at[0], sibling)

    for load in loads[:4]:
        load.wait()
    row = lax.broadcasted_iota(jnp.int32, (HALF, ROWS), 0)
    col = lax.broadcasted_iota(jnp.int32, (HALF, ROWS), 1)
    picks = [(col == 2 * row + par).astype(F32).astype(BF) for par in range(2)]

    def gather_group(two, carry):
        for par in range(2):
            which = 2 * two + par
            cols = pl.ds(pl.multiple_of(which * GW, GW), GW)
            for t in range(4):
                sq[which, t] = nn(picks[par], t_in[t, :, cols]).astype(BF)
        return carry

    lax.fori_loop(0, CTX // 2, gather_group, 0)
    out_q = []
    kept_q = None
    for dz in (0, 1, 3, 2):
        for dh in range(2):
            for kr in range(2):
                there = (half + dh) % 2
                which = (core + kr) % 2
                peer = (xx * 2 + which, (there * 2 + core) * SIDE + (zz + dz) % SIDE)
                src = sq.at[(there * 2 + which) * SIDE + (zz + dz) % SIDE]
                ss = a_ss.at[dh * 8 + dz * 2 + kr]
                rs = a_rs.at[dh * 8 + tau * 4 + dz]
                if dh or dz or kr:
                    out_q.append(send(src, rq.at[me], ss, rs, peer))
                    sent.pop()
                else:
                    kept_q = send_or_keep(at_home, src, rq.at[me], ss, rs, peer)

    loads[4].wait()
    row2 = lax.broadcasted_iota(jnp.int32, (ROWS, ROWS), 0)
    col2 = lax.broadcasted_iota(jnp.int32, (ROWS, ROWS), 1)
    wanted = jnp.where(row2 < HALF, 2 * row2 + parity, 2 * (row2 - HALF) + 1 - parity)
    permute = (col2 == wanted).astype(F32).astype(BF)

    def column(k, which, m):
        if k == 0:
            target, offset = (xx + 2) % 4, m * 128
        elif k == 3:
            target, offset = xx, m * 128
        elif m < 3:
            target, offset = (xx + 1) % 4, (k - 1) * 384 + m * 128
        else:
            target, offset = (xx + 3) % 4, (k - 1) * 384 + (m - 3) * 128
        return pl.ds(pl.multiple_of((target * 2 + which) * BLOCK + offset, 128), 128)

    kept_x = {}

    def first(k):
        z_first = SPREAD[k]
        for which in range(2):
            for n in range(TILES):
                pair = [x_in[:, column(k, which, 2 * n + e)] for e in range(2)]
                both = nn(permute, jnp.concatenate(pair, axis=1)).astype(BF)
                xs[k, which, n, 0] = both[:HALF]
                xs[k, which, n, 1] = both[HALF:]
        slot = jnp.where(at_home, 0, 4)
        for dz in (1, 3, 2, 0):
            for kr in range(2):
                which = (core + kr) % 2
                src = xs.at[k, which, 0:z_first, dz % 2]
                dst = xg.at[k, 0:z_first, slot, zz]
                i = kr * 4 + dz
                if dz or kr:
                    send(src, dst, x_ss.at[k, i], x_rs.at[k, i], dev(which, 0, dz))
                else:
                    pltpu.make_async_copy(src, dst, x_rs.at[k, i]).start()
        shift = jnp.where(at_home, 0, 1)
        for j in range(2):
            for kr in range(2):
                which = (core + kr) % 2
                dy = shift + 2 * j
                src = xs.at[k, which, z_first:TILES]
                dst = yb.at[k, 0:TILES - z_first, :, (SIDE - dy) % SIDE]
                ss, rs = x_ss.at[k, 11 + 2 * j + kr], x_rs.at[k, 11 + dy]
                if j or kr:
                    send(src, dst, ss, rs, dev(which, dy, 0))
                else:
                    kept_x[k] = send_or_keep(at_home, src, dst, ss, rs, dev(which, dy, 0))

    def second(k):
        z_first = SPREAD[k]
        rest = TILES - z_first
        for dy in range(SIDE):
            wait_in(yb.at[k, 0:rest, :, 0], x_rs.at[k, 11 + dy])
        there = xg.at[k, z_first:TILES, 0:SIDE, zz]
        for i, dz in ((15, 1), (16, 3), (17, 2)):
            src = yb.at[k, 0:rest, dz % 2]
            send(src, there, x_ss.at[k, i], x_rs.at[k, i], dev(core, 0, dz))
        pltpu.make_async_copy(yb.at[k, 0:rest, 0], there, loc_sem.at[k]).start()
        for i in range(8):
            wait_in(xg.at[k, 0:z_first, 0, 0], x_rs.at[k, i])
        for i, dy, slot in ((8, 1, 4), (9, 3, 4), (10, 2, 0)):
            src = xg.at[k, 0:z_first, slot]
            dst = xg.at[k, 0:z_first, SIDE - dy]
            send(src, dst, x_ss.at[k, i], x_rs.at[k, i], dev(core, dy, 0))

    def arrived(k):
        z_first = SPREAD[k]
        for i in (8, 9, 10):
            wait_in(xg.at[k, 0:z_first, 0], x_rs.at[k, i])
        there = xg.at[k, z_first:TILES, 0:SIDE, zz]
        wait_in(there, loc_sem.at[k])
        for i in (15, 16, 17):
            wait_in(there, x_rs.at[k, i])

    for k in range(CHUNKS):
        first(k)

    lens.wait_recv()
    own_lengths = jnp.where(at_home, len_ref[0, 0:1, 0:16], len_ref[1, 0:1, 0:16])
    rate, seg_len = rates[group], segs[group]
    ids, usable = slot_ids((SLOTS, 1), 0, parity, group, own_lengths, rate, seg_len)
    idk_ref[...] = jnp.where(usable, ids, -1)
    ids, usable = slot_ids((1, SLOTS), 1, parity, group, own_lengths, rate, seg_len)
    idq_ref[...] = jnp.where(usable, ids, -2)
    use_ref[...] = usable.astype(F32)

    second(0)
    for i in range(CTX):
        wait_in(rq.at[0], a_rs.at[i])
    for copy in out_q:
        copy.wait_send()

    @pl.when(jnp.logical_not(at_home))
    def _():
        kept_q.wait_send()

    scale = 1.0 / math.sqrt(HS)
    log2e = 1.4426950408889634

    def rolled(i):
        return pl.ds(pl.multiple_of(((i + SIDE - yy) % SIDE) * BQ, BQ), BQ)

    def heads(h, t, count):
        return rq[0:count, t, :, h * HS:(h + 1) * HS].reshape(count * HALF, HS)

    def attend(h, i):
        count = (i + 1) * (BQ // HALF)
        w = (i + 1) * BQ
        mine = slice(i * (BQ // HALF), (i + 1) * (BQ // HALF))
        cols = slice(h * HS, (h + 1) * HS)
        q = rq[mine, 0, :, cols].reshape(BQ, HS)
        g = rq[mine, 3, :, cols].reshape(BQ, HS)
        queries = slice(i * BQ, (i + 1) * BQ)
        idq = idq_ref[:, queries]
        allowed = (idk_ref[0:w] == idq) & (
            lax.broadcasted_iota(jnp.int32, (w, BQ), 0)
            <= lax.broadcasted_iota(jnp.int32, (w, BQ), 1) + i * BQ
        )
        s = jnp.where(allowed, nt(heads(h, 1, count), q) * (scale * log2e), -1e30)
        e = jnp.exp2(s - jnp.max(s, axis=0, keepdims=True))
        p = e * (use_ref[:, queries] / jnp.sum(e, axis=0, keepdims=True))
        weights = p.astype(BF)
        dprob = nt(heads(h, 2, count), g)
        delta = jnp.sum(p * dprob, axis=0, keepdims=True)
        ds = (p * (dprob - delta) * scale).astype(BF)
        out_t = nn(vt[:, 0:w], weights).astype(BF)
        gq_t = nn(kt[:, 0:w], ds).astype(BF)
        gt[core, h * HS:(h + 1) * HS, rolled(i)] = gq_t
        sq[mine, 0, :, cols] = out_t.T.reshape(BQ // HALF, HALF, HS)
        sq[mine, 1, :, cols] = gq_t.T.reshape(BQ // HALF, HALF, HS)
        gk, gv = nn(ds, q), nn(weights, g)
        if i == SLOTS // BQ - 1:
            gk_acc[...] = gk
            gv_acc[...] = gv
        else:
            gk_acc[0:w] += gk
            gv_acc[0:w] += gv

    def begin_head(h):
        kt[...] = heads(h, 1, CTX).T
        vt[...] = heads(h, 2, CTX).T

    def end_head(h):
        cols = slice(h * HS, (h + 1) * HS)
        for t, acc in ((2, gk_acc), (3, gv_acc)):
            value = acc[...].astype(BF)
            sq[:, t, :, cols] = value.reshape(CTX, HALF, HS)
            turned = value.T
            rows = slice((t - 1) * GW + h * HS, (t - 1) * GW + (h + 1) * HS)
            for i in range(SLOTS // BQ):
                gt[core, rows, rolled(i)] = turned[:, i * BQ:(i + 1) * BQ]

    between = {(0, 3): 1, (0, 0): 2, (1, 2): 3}
    for h in range(2):
        begin_head(h)
        for i in reversed(range(SLOTS // BQ)):
            attend(h, i)
            if (h, i) in between:
                second(between[(h, i)])
        end_head(h)

    grads = send(gt.at[core], gt.at[core], l_ss.at[1], l_rs.at[1], sibling)
    kept_b = None
    for dy, dz in ((0, 0), (0, 1), (1, 0), (0, 3), (3, 0), (1, 1), (3, 3), (1, 3), (3, 1),
                   (0, 2), (2, 0), (1, 2), (2, 1), (3, 2), (2, 3), (2, 2)):
        peer = dev(tau, dy, dz)
        i = dy // 2 * 8 + dz * 2
        ss, rs = b_ss.at[dy * 4 + dz], b_rs.at[i + core]
        if dy or dz:
            send(sq.at[peer[1]], back.at[group], ss, rs, peer)
        else:
            kept_b = send_or_keep(at_home, sq.at[me], back.at[group], ss, rs, peer)

    def product(k, store):
        def tile(n, carry):
            rows = xg[k, n, 0:SIDE].reshape(SLOTS, 256)
            for g in range(2):
                value = nn(gt[g], rows)
                for e in range(2):
                    store(g, n * 2 + e, value[:, e * 128:(e + 1) * 128])
            return carry

        lax.fori_loop(0, TILES, tile, 0)

    def store_far(g, u, value):
        r_far[g, u] = value.astype(BF)

    def store_near(kk):
        def store(g, u, value):
            near[kk, g, u] = value.astype(BF)
        return store

    def store_own(g, u, value):
        fin[g, u] = value

    grads.wait_recv()
    arrived(0)
    product(0, store_far)
    rel_m = send(r_far.at[0], rel.at[0], w_ss.at[0], w_rs.at[0], dev_x(3))
    rel_p = send(r_far.at[1], rel.at[1], w_ss.at[1], w_rs.at[1], dev_x(1))

    def send_near(kk, g, way):
        i = 2 + kk * 4 + way * 2
        src = near.at[kk, g, way * 3:way * 3 + 3]
        dst = rx.at[way, kk, g]
        send(src, dst, w_ss.at[i + g], w_rs.at[i + g], dev_x(3 if way else 1))

    def relay(kk):
        for u in range(3):
            near[kk, 1, u] = (near[kk, 1, u].astype(F32) + rel[1, kk * 3 + u].astype(F32)).astype(BF)
            near[kk, 0, 3 + u] = (
                near[kk, 0, 3 + u].astype(F32) + rel[0, kk * 3 + u].astype(F32)
            ).astype(BF)

    arrived(1)
    product(1, store_near(0))
    send_near(0, 0, 0)
    send_near(0, 1, 1)
    arrived(2)
    product(2, store_near(1))
    rel_m.wait_recv()
    rel_p.wait_recv()
    relay(0)
    send_near(0, 1, 0)
    send_near(0, 0, 1)
    relay(1)
    send_near(1, 1 - tau, 0)
    send_near(1, 1 - tau, 1)
    send_near(1, tau, 0)
    send_near(1, tau, 1)
    arrived(3)
    product(3, store_own)

    def gathered(kk, g):
        for way in range(2):
            i = 2 + kk * 4 + way * 2
            wait_in(rx.at[way, kk, g], w_rs.at[i + g])

    partner = dev(core, 1 - 2 * tau, 0)
    swaps = []
    for kk in range(2):
        gathered(kk, 1 - tau)
        for u in range(3):
            here = fin[1 - tau, kk * 3 + u] + rx[0, kk, 1 - tau, u].astype(F32)
            ex[kk, u] = (here + rx[1, kk, 1 - tau, u].astype(F32)).astype(BF)
        swaps.append(send(ex.at[kk], ex_in.at[kk], w_ss.at[10 + kk], w_rs.at[10 + kk], partner))
    for kk in range(2):
        gathered(kk, tau)
        for u in range(3):
            here = fin[tau, kk * 3 + u] + rx[0, kk, tau, u].astype(F32)
            fin[tau, kk * 3 + u] = here + rx[1, kk, tau, u].astype(F32)
    for kk in range(2):
        swaps[kk].wait_recv()
        for u in range(3):
            total = fin[tau, kk * 3 + u] + ex_in[kk, u].astype(F32)
            wsum[kk * 3 + u] = total * (1.0 / 128.0)

    for i in range(CTX):
        wait_in(back.at[0], b_rs.at[i])
    for copy in sent:
        copy.wait_send()

    @pl.when(jnp.logical_not(at_home))
    def _():
        kept_b.wait_send()
        for k in range(CHUNKS):
            kept_x[k].wait_send()


def finish_kernel(back, wsum, out, gq, gk, gv, weight):
    row = lax.broadcasted_iota(jnp.int32, (ROWS, HALF), 0)
    col = lax.broadcasted_iota(jnp.int32, (ROWS, HALF), 1)
    for group in range(8):
        spread = (row == 2 * col + group % 2).astype(F32).astype(BF)
        for t, ref in enumerate((out, gq, gk, gv)):
            ref[:, group * GW:(group + 1) * GW] = nn(spread, back[group, t]).astype(BF)
    for u in range(UNITS // 2):
        for j in range(3):
            weight[j, u * 128:(u + 1) * 128] = wsum[u, j * GW:(j + 1) * GW, :].T


def on_device(
    layer_input, query_rows, key_rows, value_rows, out_grad, doc_lengths, dilations, seg_lengths
):
    hbm = pl.BlockSpec(memory_space=pl.ANY)
    smem = pl.BlockSpec(memory_space=pltpu.SMEM)
    vmem = pl.BlockSpec(memory_space=pltpu.VMEM)
    dma = pltpu.SemaphoreType.DMA
    back, wsum = pl.pallas_call(
        kernel,
        out_shape=(
            jax.ShapeDtypeStruct((CTX, 4, HALF, GW), BF),
            jax.ShapeDtypeStruct((UNITS, BLOCK, 128), F32),
        ),
        in_specs=[hbm] * 5 + [vmem] + [smem] * 2,
        out_specs=(hbm, vmem),
        scratch_shapes=[
            pltpu.VMEM((ROWS, D), BF),
            pltpu.VMEM((4, ROWS, 4096), BF),
            pltpu.VMEM((2, 8, 128), jnp.int32),
            pltpu.VMEM((CTX, 4, HALF, GW), BF),
            pltpu.VMEM((CTX, 4, HALF, GW), BF),
            pltpu.VMEM((CHUNKS, 2, TILES, 2, HALF, 256), BF),
            pltpu.VMEM((CHUNKS, TILES, SIDE + 1, SIDE, HALF, 256), BF),
            pltpu.VMEM((CHUNKS, 2, 2, SIDE, HALF, 256), BF),
            pltpu.VMEM((2, 3 * GW, SLOTS), BF),
            pltpu.VMEM((SLOTS, 1), jnp.int32),
            pltpu.VMEM((1, SLOTS), jnp.int32),
            pltpu.VMEM((1, SLOTS), F32),
            pltpu.VMEM((HS, SLOTS), BF),
            pltpu.VMEM((HS, SLOTS), BF),
            pltpu.VMEM((SLOTS, HS), F32),
            pltpu.VMEM((SLOTS, HS), F32),
            pltpu.VMEM((2, UNITS, BLOCK, 128), BF),
            pltpu.VMEM((2, UNITS, BLOCK, 128), BF),
            pltpu.VMEM((2, 2, UNITS, BLOCK, 128), BF),
            pltpu.VMEM((2, 2, 2, 3, BLOCK, 128), BF),
            pltpu.VMEM((2, UNITS, BLOCK, 128), F32),
            pltpu.VMEM((2, 3, BLOCK, 128), BF),
            pltpu.VMEM((2, 3, BLOCK, 128), BF),
            dma((5,)),
            dma((CHUNKS,)),
            dma((2,)),
            dma((2,)),
            dma((CTX,)),
            dma((CTX,)),
            dma((CTX,)),
            dma((CTX,)),
            dma((CHUNKS, 18)),
            dma((CHUNKS, 18)),
            dma((12,)),
            dma((12,)),
        ],
        compiler_params=pltpu.CompilerParams(
            collective_id=0, has_side_effects=True, vmem_limit_bytes=62 * 2**20
        ),
    )(layer_input, query_rows, key_rows, value_rows, out_grad, doc_lengths, dilations, seg_lengths)
    wide = jax.ShapeDtypeStruct((ROWS, 4096), BF)
    out, gq, gk, gv, weight = pl.pallas_call(
        finish_kernel,
        grid=(2,),
        out_shape=(wide, wide, wide, wide, jax.ShapeDtypeStruct((3, BLOCK, GW), F32)),
        in_specs=[
            pl.BlockSpec((8, 4, HALF, GW), lambda i: (i, 0, 0, 0)),
            pl.BlockSpec((UNITS // 2, BLOCK, 128), lambda i: (i, 0, 0)),
        ],
        out_specs=[pl.BlockSpec((ROWS, 2048), lambda i: (0, i))] * 4
        + [pl.BlockSpec((3, BLOCK // 2, GW), lambda i: (0, i, 0))],
        compiler_params=pltpu.CompilerParams(vmem_limit_bytes=62 * 2**20),
    )(back, wsum)
    return out, gq, gk, gv, jnp.transpose(weight, (1, 0, 2))


def solution(mesh):
    rows = P(("dp", "ctx"), None)
    return jax.shard_map(
        on_device,
        mesh=mesh,
        in_specs=(rows, rows, rows, rows, rows, P("dp", None), P(), P()),
        out_specs=(rows, rows, rows, rows, P("dp", None, "ctx")),
        check_vma=False,
    )
```

time: 183 us -> 171 us (0.934)
  the two profiles are of different devices: /device:TPU:1 before, /device:TPU:104 now
where the time goes in v2:
time: 171 us; the launch traced here: 170 us
  Pallas kernels  170 us (99%)
    pallas_call x1, Pallas kernels, on_device(): pl.pallas_call(kernel, out_shape=(jax.ShapeDtypeStruct((CTX, 4, HALF, GW)...  165 us
    pallas_call x1, Pallas kernels, on_device(): pl.pallas_call(finish_kernel, grid=(2,), out_shape=(wide, wide, wide, wid...  5 us

profile of v2, /device:TPU:104, one launch (start us, length us, event | category | flops | bytes accessed | tf_op | source)
XLA Modules:
  0.0 170.5 jit_solution(5717101307277526021)
XLA Ops:
  0.6 164.8 %shard_map.119 = (bf16[16,4,64,256]{3,2,1,0:T(8,128)(2,1)}, f32[6,768,128]{2,1,0:T(8,128)}) custom-call(bf16[128,6144]{1,0:T(8,128)(2,1)} %x_hbm.1, bf16[128,4096]{1,0:T(8,128)(2,1)} %q_hbm.1, bf16[128,4096]{1,0:T(8,128)(2,1)} %k_hbm.1, bf16[128,4096]{1,0:T(8,128)(2,1)} %v_hbm.1, bf16[128,4096]{1,0:T(8,128)(2,1)} %g_hbm.1, s32[1,16]{1,0:T(1,128)} %lengths.1, ...), custom_call_target="tpu_custom_call" | custom-call | tf_op jit(solution)/shard_map/pallas_call | solution.py:448
  165.5 5.0 %shard_map.120 = (bf16[128,4096]{1,0:T(8,128)(2,1)}, bf16[128,4096]{1,0:T(8,128)(2,1)}, bf16[128,4096]{1,0:T(8,128)(2,1)}, bf16[128,4096]{1,0:T(8,128)(2,1)}, f32[3,768,256]{2,1,0:T(8,128)}) custom-call(bf16[16,4,64,256]{3,2,1,0:T(8,128)(2,1)} %get-tuple-element.12.back, f32[6,768,128]{2,1,0:T(8,128)} %get-tuple-element.13.wsum), custom_call_target="tpu_custom_call" | custom-call | tf_op jit(solution)/shard_map/pallas_call | solution.py:498

commit v3 on v2

--- a/solution.py
+++ b/solution.py
@@ -173,14 +173,16 @@
 
     kept_x = {}
 
-    def first(k):
-        z_first = SPREAD[k]
+    def prepare(k):
         for which in range(2):
             for n in range(TILES):
                 pair = [x_in[:, column(k, which, 2 * n + e)] for e in range(2)]
                 both = nn(permute, jnp.concatenate(pair, axis=1)).astype(BF)
                 xs[k, which, n, 0] = both[:HALF]
                 xs[k, which, n, 1] = both[HALF:]
+
+    def first(k):
+        z_first = SPREAD[k]
         slot = jnp.where(at_home, 0, 4)
         for dz in (1, 3, 2, 0):
             for kr in range(2):
@@ -231,8 +233,10 @@
         for i in (15, 16, 17):
             wait_in(there, x_rs.at[k, i])
 
-    for k in range(CHUNKS):
-        first(k)
+    prepare(0)
+    first(0)
+    for k in range(1, CHUNKS):
+        prepare(k)
 
     lens.wait_recv()
     own_lengths = jnp.where(at_home, len_ref[0, 0:1, 0:16], len_ref[1, 0:1, 0:16])
@@ -244,6 +248,7 @@
     use_ref[...] = usable.astype(F32)
 
     second(0)
+    first(1)
     for i in range(CTX):
         wait_in(rq.at[0], a_rs.at[i])
     for copy in out_q:
@@ -284,7 +289,7 @@
         ds = (p * (dprob - delta) * scale).astype(BF)
         out_t = nn(vt[:, 0:w], weights).astype(BF)
         gq_t = nn(kt[:, 0:w], ds).astype(BF)
-        gt[core, h * HS:(h + 1) * HS, rolled(i)] = gq_t
+        gt[core, h, 0:HS, rolled(i)] = gq_t
         sq[mine, 0, :, cols] = out_t.T.reshape(BQ // HALF, HALF, HS)
         sq[mine, 1, :, cols] = gq_t.T.reshape(BQ // HALF, HALF, HS)
         gk, gv = nn(ds, q), nn(weights, g)
@@ -305,20 +310,75 @@
             value = acc[...].astype(BF)
             sq[:, t, :, cols] = value.reshape(CTX, HALF, HS)
             turned = value.T
-            rows = slice((t - 1) * GW + h * HS, (t - 1) * GW + (h + 1) * HS)
+            rows = slice((t - 1) * HS, t * HS)
             for i in range(SLOTS // BQ):
-                gt[core, rows, rolled(i)] = turned[:, i * BQ:(i + 1) * BQ]
-
-    between = {(0, 3): 1, (0, 0): 2, (1, 2): 3}
+                gt[core, h, rows, rolled(i)] = turned[:, i * BQ:(i + 1) * BQ]
+
+    grads = []
     for h in range(2):
         begin_head(h)
         for i in reversed(range(SLOTS // BQ)):
             attend(h, i)
-            if (h, i) in between:
-                second(between[(h, i)])
         end_head(h)
-
-    grads = send(gt.at[core], gt.at[core], l_ss.at[1], l_rs.at[1], sibling)
+        grads.append(send(gt.at[core, h], gt.at[core, h], l_ss.at[1 + h], l_rs.at[1 + h], sibling))
+
+    def product(k, store):
+        def tile(n, carry):
+            rows = xg[k, n, 0:SIDE].reshape(SLOTS, 256)
+            for g in range(2):
+                value = nn(gt[g].reshape(3 * GW, SLOTS), rows)
+                for e in range(2):
+                    store(g, n * 2 + e, value[:, e * 128:(e + 1) * 128])
+            return carry
+
+        lax.fori_loop(0, TILES, tile, 0)
+
+    def store_far(g, u, value):
+        r_far[g, u] = value.astype(BF)
+
+    def store_near(kk):
+        def store(g, u, value):
+            near[kk, g, u] = value.astype(BF)
+        return store
+
+    def store_own(g, u, value):
+        fin[g, u] = value
+
+    for copy in grads:
+        copy.wait_recv()
+    arrived(0)
+    product(0, store_far)
+    rel_m = send(r_far.at[0], rel.at[0], w_ss.at[0], w_rs.at[0], dev_x(3))
+    rel_p = send(r_far.at[1], rel.at[1], w_ss.at[1], w_rs.at[1], dev_x(1))
+
+    second(1)
+    first(2)
+    first(3)
+
+    def send_near(kk, g, way):
+        i = 2 + kk * 4 + way * 2
+        src = near.at[kk, g, way * 3:way * 3 + 3]
+        dst = rx.at[way, kk, g]
+        send(src, dst, w_ss.at[i + g], w_rs.at[i + g], dev_x(3 if way else 1))
+
+    def relay(kk):
+        for u in range(3):
+            near[kk, 1, u] = (near[kk, 1, u].astype(F32) + rel[1, kk * 3 + u].astype(F32)).astype(BF)
+            near[kk, 0, 3 + u] = (
+                near[kk, 0, 3 + u].astype(F32) + rel[0, kk * 3 + u].astype(F32)
+            ).astype(BF)
+
+    arrived(1)
+    product(1, store_near(0))
+    send_near(0, 0, 0)
+    send_near(0, 1, 1)
+    second(2)
+    second(3)
+    rel_m.wait_recv()
+    rel_p.wait_recv()
+    relay(0)
+    send_near(0, 1, 0)
+    send_near(0, 0, 1)
     kept_b = None
     for dy, dz in ((0, 0), (0, 1), (1, 0), (0, 3), (3, 0), (1, 1), (3, 3), (1, 3), (3, 1),
                    (0, 2), (2, 0), (1, 2), (2, 1), (3, 2), (2, 3), (2, 2)):
@@ -330,58 +390,8 @@
         else:
             kept_b = send_or_keep(at_home, sq.at[me], back.at[group], ss, rs, peer)
 
-    def product(k, store):
-        def tile(n, carry):
-            rows = xg[k, n, 0:SIDE].reshape(SLOTS, 256)
-            for g in range(2):
-                value = nn(gt[g], rows)
-                for e in range(2):
-                    store(g, n * 2 + e, value[:, e * 128:(e + 1) * 128])
-            return carry
-
-        lax.fori_loop(0, TILES, tile, 0)
-
-    def store_far(g, u, value):
-        r_far[g, u] = value.astype(BF)
-
-    def store_near(kk):
-        def store(g, u, value):
-            near[kk, g, u] = value.astype(BF)
-        return store
-
-    def store_own(g, u, value):
-        fin[g, u] = value
-
-    grads.wait_recv()
-    arrived(0)
-    product(0, store_far)
-    rel_m = send(r_far.at[0], rel.at[0], w_ss.at[0], w_rs.at[0], dev_x(3))
-    rel_p = send(r_far.at[1], rel.at[1], w_ss.at[1], w_rs.at[1], dev_x(1))
-
-    def send_near(kk, g, way):
-        i = 2 + kk * 4 + way * 2
-        src = near.at[kk, g, way * 3:way * 3 + 3]
-        dst = rx.at[way, kk, g]
-        send(src, dst, w_ss.at[i + g], w_rs.at[i + g], dev_x(3 if way else 1))
-
-    def relay(kk):
-        for u in range(3):
-            near[kk, 1, u] = (near[kk, 1, u].astype(F32) + rel[1, kk * 3 + u].astype(F32)).astype(BF)
-            near[kk, 0, 3 + u] = (
-                near[kk, 0, 3 + u].astype(F32) + rel[0, kk * 3 + u].astype(F32)
-            ).astype(BF)
-
-    arrived(1)
-    product(1, store_near(0))
-    send_near(0, 0, 0)
-    send_near(0, 1, 1)
     arrived(2)
     product(2, store_near(1))
-    rel_m.wait_recv()
-    rel_p.wait_recv()
-    relay(0)
-    send_near(0, 1, 0)
-    send_near(0, 0, 1)
     relay(1)
     send_near(1, 1 - tau, 0)
     send_near(1, 1 - tau, 1)
@@ -435,7 +445,9 @@
             ref[:, group * GW:(group + 1) * GW] = nn(spread, back[group, t]).astype(BF)
     for u in range(UNITS // 2):
         for j in range(3):
-            weight[j, u * 128:(u + 1) * 128] = wsum[u, j * GW:(j + 1) * GW, :].T
+            for h in range(2):
+                rows = slice((h * 3 + j) * HS, (h * 3 + j + 1) * HS)
+                weight[j, u * 128:(u + 1) * 128, h * HS:(h + 1) * HS] = wsum[u, rows, :].T
 
 
 def on_device(
@@ -462,7 +474,7 @@
             pltpu.VMEM((CHUNKS, 2, TILES, 2, HALF, 256), BF),
             pltpu.VMEM((CHUNKS, TILES, SIDE + 1, SIDE, HALF, 256), BF),
             pltpu.VMEM((CHUNKS, 2, 2, SIDE, HALF, 256), BF),
-            pltpu.VMEM((2, 3 * GW, SLOTS), BF),
+            pltpu.VMEM((2, 2, 3 * HS, SLOTS), BF),
             pltpu.VMEM((SLOTS, 1), jnp.int32),
             pltpu.VMEM((1, SLOTS), jnp.int32),
             pltpu.VMEM((1, SLOTS), F32),
@@ -479,8 +491,8 @@
             pltpu.VMEM((2, 3, BLOCK, 128), BF),
             dma((5,)),
             dma((CHUNKS,)),
-            dma((2,)),
-            dma((2,)),
+            dma((3,)),
+            dma((3,)),
             dma((CTX,)),
             dma((CTX,)),
             dma((CTX,)),

time: 171 us -> 158 us (0.924)
  the two profiles are of different devices: /device:TPU:104 before, /device:TPU:48 now
where the time goes in v3:
time: 158 us
  Pallas kernels  157 us (99%)
    pallas_call x1, Pallas kernels, on_device(): pl.pallas_call(kernel, out_shape=(jax.ShapeDtypeStruct((CTX, 4, HALF, GW)...  152 us
    pallas_call x1, Pallas kernels, on_device(): pl.pallas_call(finish_kernel, grid=(2,), out_shape=(wide, wide, wide, wid...  5 us

profile of v3, /device:TPU:48, one launch (start us, length us, event | category | flops | bytes accessed | tf_op | source)
XLA Modules:
  0.0 157.6 jit_solution(17722334593995996429)
XLA Ops:
  0.6 151.9 %shard_map.119 = (bf16[16,4,64,256]{3,2,1,0:T(8,128)(2,1)}, f32[6,768,128]{2,1,0:T(8,128)}) custom-call(bf16[128,6144]{1,0:T(8,128)(2,1)} %x_hbm.1, bf16[128,4096]{1,0:T(8,128)(2,1)} %q_hbm.1, bf16[128,4096]{1,0:T(8,128)(2,1)} %k_hbm.1, bf16[128,4096]{1,0:T(8,128)(2,1)} %v_hbm.1, bf16[128,4096]{1,0:T(8,128)(2,1)} %g_hbm.1, s32[1,16]{1,0:T(1,128)} %lengths.1, ...), custom_call_target="tpu_custom_call" | custom-call | tf_op jit(solution)/shard_map/pallas_call | solution.py:460
  152.6 5.0 %shard_map.120 = (bf16[128,4096]{1,0:T(8,128)(2,1)}, bf16[128,4096]{1,0:T(8,128)(2,1)}, bf16[128,4096]{1,0:T(8,128)(2,1)}, bf16[128,4096]{1,0:T(8,128)(2,1)}, f32[3,768,256]{2,1,0:T(8,128)}) custom-call(bf16[16,4,64,256]{3,2,1,0:T(8,128)(2,1)} %get-tuple-element.12.back, f32[6,768,128]{2,1,0:T(8,128)} %get-tuple-element.13.wsum), custom_call_target="tpu_custom_call" | custom-call | tf_op jit(solution)/shard_map/pallas_call | solution.py:510

commit v4 on v3

--- a/solution.py
+++ b/solution.py
@@ -136,23 +136,26 @@
                 sq[which, t] = nn(picks[par], t_in[t, :, cols]).astype(BF)
         return carry
 
-    lax.fori_loop(0, CTX // 2, gather_group, 0)
     out_q = []
     kept_q = None
-    for dz in (0, 1, 3, 2):
-        for dh in range(2):
-            for kr in range(2):
-                there = (half + dh) % 2
-                which = (core + kr) % 2
-                peer = (xx * 2 + which, (there * 2 + core) * SIDE + (zz + dz) % SIDE)
-                src = sq.at[(there * 2 + which) * SIDE + (zz + dz) % SIDE]
-                ss = a_ss.at[dh * 8 + dz * 2 + kr]
-                rs = a_rs.at[dh * 8 + tau * 4 + dz]
-                if dh or dz or kr:
-                    out_q.append(send(src, rq.at[me], ss, rs, peer))
-                    sent.pop()
-                else:
-                    kept_q = send_or_keep(at_home, src, rq.at[me], ss, rs, peer)
+    for dh, order in enumerate((
+        ((1, 0), (3, 1), (2, 0), (1, 1), (3, 0), (2, 1), (0, 1), (0, 0)),
+        ((0, 1), (1, 0), (3, 1), (0, 0), (1, 1), (3, 0), (2, 0), (2, 1)),
+    )):
+        base = ((half + dh) % 2) * (CTX // 4)
+        lax.fori_loop(base, base + CTX // 4, gather_group, 0)
+        for dz, kr in order:
+            there = (half + dh) % 2
+            which = (core + kr) % 2
+            peer = (xx * 2 + which, (there * 2 + core) * SIDE + (zz + dz) % SIDE)
+            src = sq.at[(there * 2 + which) * SIDE + (zz + dz) % SIDE]
+            ss = a_ss.at[dh * 8 + dz * 2 + kr]
+            rs = a_rs.at[dh * 8 + tau * 4 + dz]
+            if dh or dz or kr:
+                out_q.append(send(src, rq.at[me], ss, rs, peer))
+                sent.pop()
+            else:
+                kept_q = send_or_keep(at_home, src, rq.at[me], ss, rs, peer)
 
     loads[4].wait()
     row2 = lax.broadcasted_iota(jnp.int32, (ROWS, ROWS), 0)
@@ -249,6 +252,8 @@
 
     second(0)
     first(1)
+    first(2)
+    first(3)
     for i in range(CTX):
         wait_in(rq.at[0], a_rs.at[i])
     for copy in out_q:
@@ -352,14 +357,14 @@
     rel_p = send(r_far.at[1], rel.at[1], w_ss.at[1], w_rs.at[1], dev_x(1))
 
     second(1)
-    first(2)
-    first(3)
+    second(2)
+    second(3)
 
     def send_near(kk, g, way):
         i = 2 + kk * 4 + way * 2
-        src = near.at[kk, g, way * 3:way * 3 + 3]
+        src = near.at[kk, g, pl.ds(way * 3, 3)]
         dst = rx.at[way, kk, g]
-        send(src, dst, w_ss.at[i + g], w_rs.at[i + g], dev_x(3 if way else 1))
+        send(src, dst, w_ss.at[i + g], w_rs.at[i + g], dev_x(1 + 2 * way))
 
     def relay(kk):
         for u in range(3):
@@ -368,17 +373,14 @@
                 near[kk, 0, 3 + u].astype(F32) + rel[0, kk * 3 + u].astype(F32)
             ).astype(BF)
 
+    other = 1 - tau
     arrived(1)
     product(1, store_near(0))
-    send_near(0, 0, 0)
-    send_near(0, 1, 1)
-    second(2)
-    second(3)
+    send_near(0, other, other)
     rel_m.wait_recv()
     rel_p.wait_recv()
     relay(0)
-    send_near(0, 1, 0)
-    send_near(0, 0, 1)
+    send_near(0, other, tau)
     kept_b = None
     for dy, dz in ((0, 0), (0, 1), (1, 0), (0, 3), (3, 0), (1, 1), (3, 3), (1, 3), (3, 1),
                    (0, 2), (2, 0), (1, 2), (2, 1), (3, 2), (2, 3), (2, 2)):
@@ -393,10 +395,9 @@
     arrived(2)
     product(2, store_near(1))
     relay(1)
-    send_near(1, 1 - tau, 0)
-    send_near(1, 1 - tau, 1)
-    send_near(1, tau, 0)
-    send_near(1, tau, 1)
+    for kk, g in ((1, other), (0, tau), (1, tau)):
+        for way in range(2):
+            send_near(kk, g, way)
     arrived(3)
     product(3, store_own)
 

time: 158 us -> 149 us (0.943)
  the two profiles are of different devices: /device:TPU:48 before, /device:TPU:8 now
where the time goes in v4:
time: 149 us; the launch traced here: 146 us
  Pallas kernels  146 us (98%)
    pallas_call x1, Pallas kernels, on_device(): pl.pallas_call(kernel, out_shape=(jax.ShapeDtypeStruct((CTX, 4, HALF, GW)...  141 us
    pallas_call x1, Pallas kernels, on_device(): pl.pallas_call(finish_kernel, grid=(2,), out_shape=(wide, wide, wide, wid...  5 us

profile of v4, /device:TPU:8, one launch (start us, length us, event | category | flops | bytes accessed | tf_op | source)
XLA Modules:
  0.0 146.4 jit_solution(15180130240355726590)
XLA Ops:
  0.6 140.8 %shard_map.119 = (bf16[16,4,64,256]{3,2,1,0:T(8,128)(2,1)}, f32[6,768,128]{2,1,0:T(8,128)}) custom-call(bf16[128,6144]{1,0:T(8,128)(2,1)} %x_hbm.1, bf16[128,4096]{1,0:T(8,128)(2,1)} %q_hbm.1, bf16[128,4096]{1,0:T(8,128)(2,1)} %k_hbm.1, bf16[128,4096]{1,0:T(8,128)(2,1)} %v_hbm.1, bf16[128,4096]{1,0:T(8,128)(2,1)} %g_hbm.1, s32[1,16]{1,0:T(1,128)} %lengths.1, ...), custom_call_target="tpu_custom_call" | custom-call | tf_op jit(solution)/shard_map/pallas_call | solution.py:461
  141.4 5.0 %shard_map.120 = (bf16[128,4096]{1,0:T(8,128)(2,1)}, bf16[128,4096]{1,0:T(8,128)(2,1)}, bf16[128,4096]{1,0:T(8,128)(2,1)}, bf16[128,4096]{1,0:T(8,128)(2,1)}, f32[3,768,256]{2,1,0:T(8,128)}) custom-call(bf16[16,4,64,256]{3,2,1,0:T(8,128)(2,1)} %get-tuple-element.12.back, f32[6,768,128]{2,1,0:T(8,128)} %get-tuple-element.13.wsum), custom_call_target="tpu_custom_call" | custom-call | tf_op jit(solution)/shard_map/pallas_call | solution.py:511

commit v5 on v4

--- a/solution.py
+++ b/solution.py
@@ -327,10 +327,10 @@
         end_head(h)
         grads.append(send(gt.at[core, h], gt.at[core, h], l_ss.at[1 + h], l_rs.at[1 + h], sibling))
 
-    def product(k, store):
+    def product(k, store, groups=(0, 1)):
         def tile(n, carry):
             rows = xg[k, n, 0:SIDE].reshape(SLOTS, 256)
-            for g in range(2):
+            for g in groups:
                 value = nn(gt[g].reshape(3 * GW, SLOTS), rows)
                 for e in range(2):
                     store(g, n * 2 + e, value[:, e * 128:(e + 1) * 128])
@@ -349,12 +349,15 @@
     def store_own(g, u, value):
         fin[g, u] = value
 
-    for copy in grads:
-        copy.wait_recv()
     arrived(0)
-    product(0, store_far)
-    rel_m = send(r_far.at[0], rel.at[0], w_ss.at[0], w_rs.at[0], dev_x(3))
-    rel_p = send(r_far.at[1], rel.at[1], w_ss.at[1], w_rs.at[1], dev_x(1))
+    rels = []
+    for g in (core, 1 - core):
+        if rels:
+            for copy in grads:
+                copy.wait_recv()
+        product(0, store_far, (g,))
+        to = dev_x(jnp.where(g == 0, 3, 1))
+        rels.append(send(r_far.at[g], rel.at[g], w_ss.at[g], w_rs.at[g], to))
 
     second(1)
     second(2)
@@ -377,10 +380,6 @@
     arrived(1)
     product(1, store_near(0))
     send_near(0, other, other)
-    rel_m.wait_recv()
-    rel_p.wait_recv()
-    relay(0)
-    send_near(0, other, tau)
     kept_b = None
     for dy, dz in ((0, 0), (0, 1), (1, 0), (0, 3), (3, 0), (1, 1), (3, 3), (1, 3), (3, 1),
                    (0, 2), (2, 0), (1, 2), (2, 1), (3, 2), (2, 3), (2, 2)):
@@ -392,6 +391,10 @@
         else:
             kept_b = send_or_keep(at_home, sq.at[me], back.at[group], ss, rs, peer)
 
+    for copy in rels:
+        copy.wait_recv()
+    relay(0)
+    send_near(0, other, tau)
     arrived(2)
     product(2, store_near(1))
     relay(1)
@@ -416,14 +419,11 @@
         swaps.append(send(ex.at[kk], ex_in.at[kk], w_ss.at[10 + kk], w_rs.at[10 + kk], partner))
     for kk in range(2):
         gathered(kk, tau)
+        swaps[kk].wait_recv()
         for u in range(3):
             here = fin[tau, kk * 3 + u] + rx[0, kk, tau, u].astype(F32)
-            fin[tau, kk * 3 + u] = here + rx[1, kk, tau, u].astype(F32)
-    for kk in range(2):
-        swaps[kk].wait_recv()
-        for u in range(3):
-            total = fin[tau, kk * 3 + u] + ex_in[kk, u].astype(F32)
-            wsum[kk * 3 + u] = total * (1.0 / 128.0)
+            here = here + rx[1, kk, tau, u].astype(F32) + ex_in[kk, u].astype(F32)
+            wsum[kk * 3 + u] = here * (1.0 / 128.0)
 
     for i in range(CTX):
         wait_in(back.at[0], b_rs.at[i])

time: 149 us -> 148 us (level)
  no operation moved by 1% of the time
where the time goes in v5:
time: 148 us; the launch traced here: 147 us
  Pallas kernels  146 us (99%)
    pallas_call x1, Pallas kernels, on_device(): pl.pallas_call(kernel, out_shape=(jax.ShapeDtypeStruct((CTX, 4, HALF, GW)...  141 us
    pallas_call x1, Pallas kernels, on_device(): pl.pallas_call(finish_kernel, grid=(2,), out_shape=(wide, wide, wide, wid...  5.01 us

profile of v5, /device:TPU:8, one launch (start us, length us, event | category | flops | bytes accessed | tf_op | source)
XLA Modules:
  0.0 146.5 jit_solution(10288215141991266679)
XLA Ops:
  0.6 140.9 %shard_map.119 = (bf16[16,4,64,256]{3,2,1,0:T(8,128)(2,1)}, f32[6,768,128]{2,1,0:T(8,128)}) custom-call(bf16[128,6144]{1,0:T(8,128)(2,1)} %x_hbm.1, bf16[128,4096]{1,0:T(8,128)(2,1)} %q_hbm.1, bf16[128,4096]{1,0:T(8,128)(2,1)} %k_hbm.1, bf16[128,4096]{1,0:T(8,128)(2,1)} %v_hbm.1, bf16[128,4096]{1,0:T(8,128)(2,1)} %g_hbm.1, s32[1,16]{1,0:T(1,128)} %lengths.1, ...), custom_call_target="tpu_custom_call" | custom-call | tf_op jit(solution)/shard_map/pallas_call | solution.py:461
  141.5 5.0 %shard_map.120 = (bf16[128,4096]{1,0:T(8,128)(2,1)}, bf16[128,4096]{1,0:T(8,128)(2,1)}, bf16[128,4096]{1,0:T(8,128)(2,1)}, bf16[128,4096]{1,0:T(8,128)(2,1)}, f32[3,768,256]{2,1,0:T(8,128)}) custom-call(bf16[16,4,64,256]{3,2,1,0:T(8,128)(2,1)} %get-tuple-element.12.back, f32[6,768,128]{2,1,0:T(8,128)} %get-tuple-element.13.wsum), custom_call_target="tpu_custom_call" | custom-call | tf_op jit(solution)/shard_map/pallas_call | solution.py:511
